TPU v7x, 512 devices: a whole 4x8x8 slice. The times are simulated.
512 devices in a mesh: gz: 32 (over x, z), gx: 8 (over y), gy: 2 (over core).
Axes of the slice: x: 4, y: 8, z: 8, core: 2. Of those that a mesh axis runs over, the one named last changes fastest.
Arguments:
- solution_in: float32 [768, 64, 256], P('gz', 'gx', 'gy'), may hold values from -6 to 6
- residual_in: float32 [768, 64, 256], P('gz', 'gx', 'gy'), may hold values from -13 to 13
- direction_in: float32 [768, 64, 256], P('gz', 'gx', 'gy'), may hold values from -17 to 17
- cond_x: float32 [768, 64, 256], P('gz', 'gx', 'gy'), may hold values from 0.05 to 0.5
- cond_y: float32 [768, 64, 256], P('gz', 'gx', 'gy'), may hold values from 0.05 to 0.5
- cond_z: float32 [768, 64, 256], P('gz', 'gx', 'gy'), may hold values from 1500 to 6000
- helmholtz: float32 [768, 64, 256], P('gz', 'gx', 'gy'), may hold values from 0.1 to 0.6
Outputs:
- solution_out: float32 [768, 64, 256], P('gz', 'gx', 'gy')
- residual_out: float32 [768, 64, 256], P('gz', 'gx', 'gy')
- direction_out: float32 [768, 64, 256], P('gz', 'gx', 'gy')
All inputs are finite; a program needn't handle non-finite values.
Results may differ from a plain program's by a relative error of at most 0.00035.
Values sent between devices are 32-bit elements; how exact they have to be, the bound alone decides.
No kernel may reach another device: no remote copies, remote signals or barrier semaphores. Data moves between devices by JAX's collectives and lax.ppermute only.
A program may use at most 64 MiB of HBM per device.

v0:
```python
import jax
import jax.numpy as jnp
from jax import lax
from jax.sharding import PartitionSpec as P


def with_halo(cells, sides, width):
    for axis, dim in sides:
        count = lax.axis_size(axis)
        ends = count - 1
        head = lax.slice_in_dim(cells, 0, width, axis=dim)
        tail = lax.slice_in_dim(cells, cells.shape[dim] - width, cells.shape[dim], axis=dim)
        cells = jnp.concatenate(
            [
                lax.ppermute(tail, axis, [(i, (i + 1) % count) for i in range(ends)]),
                cells,
                lax.ppermute(head, axis, [((i + 1) % count, i) for i in range(ends)]),
            ],
            axis=dim,
        )
    return cells


def passed_along(value, axis, by):
    length = lax.axis_size(axis)
    pairs = [(i, i + by) for i in range(length) if 0 <= i + by < length]
    return lax.ppermute(value, axis, pairs)


def stencil(padded, values, coeffs):
    cond_x, cond_y, cond_z, low_x, low_y, low_z, diagonal = coeffs
    result = diagonal * values - cond_x * padded[1:-1, 2:, 1:-1] - low_x * padded[1:-1, :-2, 1:-1]
    result = result - cond_y * padded[1:-1, 1:-1, 2:] - low_y * padded[1:-1, 1:-1, :-2]
    return result - cond_z * padded[2:, 1:-1, 1:-1] - low_z * padded[:-2, 1:-1, 1:-1]


def operate(values, coeffs):
    padded = with_halo(values, (("gz", 0), ("gx", 1), ("gy", 2)), 1)
    return stencil(padded, values, coeffs)


def tridiagonal(lower_coef, main_coef, upper_coef, source):

    def forward(running, row_set):
        ratio_prev, shift_prev = running
        low_row, main_row, up_row, src_row = row_set
        divisor = main_row - low_row * ratio_prev
        ratio_next = up_row / divisor
        shift_next = (src_row - low_row * shift_prev) / divisor
        return ((ratio_next, shift_next), (ratio_next, shift_next))

    zeros_row = jnp.zeros(main_coef.shape[1:], jnp.float32)
    ignored, (ratios, shifts) = lax.scan(
        forward, (zeros_row, zeros_row), (lower_coef, main_coef, upper_coef, source)
    )

    def backward(after_value, row_set):
        ratio_row, shift_row = row_set
        solved = shift_row - ratio_row * after_value
        return (solved, solved)

    ignored, solved_rows = lax.scan(backward, zeros_row, (ratios, shifts), reverse=True)
    return solved_rows


def interior_solve(diagonal, cond_z, low_z, residual):
    row_count = diagonal.shape[0]
    zeros_row = jnp.zeros(diagonal.shape[1:], jnp.float32)
    ratio_prev = zeros_row
    shift_prev = jnp.zeros((3,) + diagonal.shape[1:], jnp.float32)
    ratios = []
    shifts = []
    for row_at in range(1, row_count):
        low_row = -low_z[row_at]
        divisor = diagonal[row_at] - low_row * ratio_prev
        ratio_prev = -cond_z[row_at] / divisor
        first_src = cond_z[0] if row_at == 1 else zeros_row
        last_src = cond_z[row_count - 1] if row_at == row_count - 1 else zeros_row
        source = jnp.stack([residual[row_at], first_src, last_src])
        shift_prev = (source - low_row * shift_prev) / divisor
        ratios.append(ratio_prev)
        shifts.append(shift_prev)
    solved = shifts[-1]
    collected = [solved]
    for row_at in range(len(shifts) - 2, -1, -1):
        solved = shifts[row_at] - ratios[row_at] * solved
        collected.append(solved)
    return jnp.stack(collected[::-1], axis=1)


def body(solution_in, residual_in, direction_in, cond_x, cond_y, cond_z, helmholtz):
    stacked = jnp.stack([direction_in, cond_x, cond_y, cond_z])
    padded = with_halo(stacked, (("gz", 1), ("gx", 2), ("gy", 3)), 1)
    low_x = padded[1, 1:-1, :-2, 1:-1]
    low_y = padded[2, 1:-1, 1:-1, :-2]
    low_z = padded[3, :-2, 1:-1, 1:-1]
    direction_padded = padded[0]
    diagonal = helmholtz + cond_x + low_x + cond_y + low_y + cond_z + low_z
    coeffs = (cond_x, cond_y, cond_z, low_x, low_y, low_z, diagonal)
    image_old = stencil(direction_padded, direction_in, coeffs)
    local_parts = interior_solve(diagonal, cond_z, low_z, residual_in)
    base_part = local_parts[0]
    first_part = local_parts[1]
    last_part = local_parts[2]
    top_rows = jnp.stack([base_part[-1], first_part[-1], last_part[-1]])
    beneath = passed_along(top_rows, "gz", 1)
    face_below = low_z[0]
    face_above = cond_z[0]
    lower_coef = -face_below * beneath[1]
    main_coef = diagonal[0] - face_below * beneath[2] - face_above * first_part[0]
    upper_coef = -face_above * last_part[0]
    source_coef = residual_in[0] + face_below * beneath[0] + face_above * base_part[0]
    gathered = lax.all_gather(
        jnp.stack([lower_coef, main_coef, upper_coef, source_coef])[None], "gz", axis=0, tiled=True
    )
    solved_all = tridiagonal(gathered[:, 0], gathered[:, 1], gathered[:, 2], gathered[:, 3])
    position = lax.axis_index("gz")
    extended = jnp.concatenate([solved_all, jnp.zeros_like(solved_all[:1])], axis=0)
    first_own = lax.dynamic_index_in_dim(extended, position, 0, keepdims=False)
    first_next = lax.dynamic_index_in_dim(extended, position + 1, 0, keepdims=False)
    interior = base_part + first_own[None] * first_part + first_next[None] * last_part
    precond = jnp.concatenate([first_own[None], interior], axis=0)
    along_image, old_image = lax.psum(
        (jnp.sum(precond * image_old), jnp.sum(direction_in * image_old)), ("gz", "gx", "gy")
    )
    conj = -along_image / old_image
    direction_out = precond + conj * direction_in
    image = operate(direction_out, coeffs)
    numer, denom_sum = lax.psum(
        (jnp.sum(residual_in * direction_out), jnp.sum(direction_out * image)), ("gz", "gx", "gy")
    )
    step_size = numer / denom_sum
    return (solution_in + step_size * direction_out, residual_in - step_size * image, direction_out)


def solution(mesh):
    in_specs = (
        P("gz", "gx", "gy"),
        P("gz", "gx", "gy"),
        P("gz", "gx", "gy"),
        P("gz", "gx", "gy"),
        P("gz", "gx", "gy"),
        P("gz", "gx", "gy"),
        P("gz", "gx", "gy"),
    )
    out_specs = (P("gz", "gx", "gy"), P("gz", "gx", "gy"), P("gz", "gx", "gy"))
    return jax.shard_map(body, mesh=mesh, in_specs=in_specs, out_specs=out_specs, check_vma=False)
```

profile of v0, /device:TPU:1, one launch (start us, length us, event | category | flops | bytes accessed | tf_op | source)
XLA Modules:
  0.0 324.1 jit_solution(10633019987609649447)
XLA Ops:
  1.5 4.8 %collective-permute-start = (f32[4,1,8,128]{3,2,1,0:T(8,128)S(1)}, f32[4,1,8,128]{3,2,1,0:T(8,128)S(1)}, u32[]{:S(2)}, u32[]{:S(2)}) collective-permute-start(f32[4,1,8,128]{3,2,1,0:T(8,128)S(1)} %get-tuple-element.320), channel_id=1, source_target_pairs={{0,16},{16,32},{32,48},{48,64},{64,80},{80,96},{96,112},{112,128},... | collective-permute-start | bytes 49160 | tf_op jit(solution)/shard_map/ppermute | solution.py:15
  6.4 1.3 collective-permute-start.1
  10.2 1.3 collective-permute-done.1
  11.5 1.3 pad_maximum_fusion.49
  12.8 3.2 collective-permute-start.2
  16.0 1.3 collective-permute-start.3
  17.3 2.7 pad_maximum_fusion.1
  21.7 1.3 collective-permute-start.4
  23.4 5.1 %collective-permute-start.6 = (f32[4,26,10,1]{1,0,3,2:T(4,128)S(1)}, f32[4,26,10,1]{1,0,3,2:T(4,128)S(1)}, u32[]{:S(2)}, u32[]{:S(2)}) collective-permute-start(f32[4,26,10,1]{1,0,3,2:T(4,128)S(1)} %copy.126), channel_id=1, source_target_pairs={{1,0},{3,2},{5,4},{7,6},{9,8},{11,10},{13,12},{15,14},{17,16},{19,... | collective-permute-start | bytes 12488 | tf_op jit(solution)/shard_map/ppermute | solution.py:17
  28.6 1.6 pad_maximum_fusion
  34.4 4.0 %collective-permute-start.5 = (f32[3,8,128]{2,1,0:T(8,128)S(1)}, f32[3,8,128]{2,1,0:T(8,128)S(1)}, u32[]{:S(2)}, u32[]{:S(2)}) collective-permute-start(f32[3,8,128]{2,1,0:T(8,128)S(1)} %get-tuple-element.267), channel_id=1, source_target_pairs={{0,16},{16,32},{32,48},{48,64},{64,80},{80,96},{96,112},{112,128},... | collective-permute-start | bytes 36872 | tf_op jit(solution)/shard_map/ppermute | solution.py:27
  39.2 44.0 %all-gather = f32[128,8,128]{2,1,0:T(8,128)S(1)} all-gather(f32[4,8,128]{2,1,0:T(8,128)S(1)} %pad_maximum_fusion.54), channel_id=2, replica_groups=mesh['gz'=32,'gx'=8,'gy'=2] {'gz'}, dimensions={0}, use_global_device_ids=true | all-gather | bytes 540672 | tf_op jit(solution)/shard_map/all_gather | solution.py:113
  83.2 1.3 while.34
  86.4 108.1 %all-reduce.23 = (f32[]{:T(128)}, f32[]{:T(128)}) all-reduce(f32[]{:T(128)} %get-tuple-element.211, f32[]{:T(128)} %get-tuple-element.210), channel_id=1, replica_groups=mesh['gz'=32,'gx'=8,'gy'=2] {'gz','gx','gy'}, use_global_device_ids=true, to_apply=%region_5.6 | all-reduce | flops 2 | bytes 16 | tf_op jit(solution)/shard_map/psum | solution.py:123
  195.9 2.4 collective-permute-start.7
  198.3 1.3 collective-permute-start.8
  199.6 3.0 collective-permute-done.8
  202.7 2.7 collective-permute-start.10
  205.4 1.3 collective-permute-start.9
  206.7 3.4 %collective-permute-done.9 = f32[26,1,128]{2,1,0:T(1,128)S(1)} collective-permute-done((f32[26,1,128]{2,1,0:T(1,128)S(1)}, f32[26,1,128]{2,1,0:T(1,128)S(1)}, u32[]{:S(2)}, u32[]{:S(2)}) %collective-permute-start.9) | collective-permute-done | bytes 13344 | tf_op jit(solution)/shard_map/ppermute | solution.py:17
  210.4 5.5 %collective-permute-start.11 = (f32[26,10,1]{2,1,0:T(8,128)S(1)}, f32[26,10,1]{2,1,0:T(8,128)S(1)}, u32[]{:S(2)}, u32[]{:S(2)}) collective-permute-start(f32[26,10,1]{2,1,0:T(8,128)S(1)} %get-tuple-element.324), channel_id=1, source_target_pairs={{1,0},{3,2},{5,4},{7,6},{9,8},{11,10},{13,12},{15,14},{17,16},{19,... | collective-permute-start | bytes 3128 | tf_op jit(solution)/shard_map/ppermute | solution.py:17
  215.8 1.3 collective-permute-start.12
  217.2 2.0 collective-permute-done.12
  220.0 101.4 %all-reduce.22 = (f32[]{:T(128)}, f32[]{:T(128)}) all-reduce(f32[]{:T(128)} %get-tuple-element.209, f32[]{:T(128)} %get-tuple-element.208), channel_id=1, replica_groups=mesh['gz'=32,'gx'=8,'gy'=2] {'gz','gx','gy'}, use_global_device_ids=true, to_apply=%region_9.10 | all-reduce | flops 2 | bytes 16 | tf_op jit(solution)/shard_map/psum | solution.py:129
  (160 shorter events, 15.3 us)
Async XLA Ops:
  0.6 20.2 %copy-start = (f32[24,8,128]{2,1,0:T(8,128)S(1)}, f32[24,8,128]{2,1,0:T(8,128)}, u32[]{:S(2)}) copy-start(f32[24,8,128]{2,1,0:T(8,128)} %param.16) | copy-start | bytes 294916
  0.6 20.2 %copy-start.1 = (f32[24,8,128]{2,1,0:T(8,128)S(1)}, f32[24,8,128]{2,1,0:T(8,128)}, u32[]{:S(2)}) copy-start(f32[24,8,128]{2,1,0:T(8,128)} %param.15) | copy-start | bytes 294916
  0.7 20.2 %copy-start.2 = (f32[24,8,128]{2,1,0:T(8,128)S(1)}, f32[24,8,128]{2,1,0:T(8,128)}, u32[]{:S(2)}) copy-start(f32[24,8,128]{2,1,0:T(8,128)} %param.14) | copy-start | bytes 294916
  0.7 20.2 %copy-start.3 = (f32[24,8,128]{2,1,0:T(8,128)S(1)}, f32[24,8,128]{2,1,0:T(8,128)}, u32[]{:S(2)}) copy-start(f32[24,8,128]{2,1,0:T(8,128)} %param.13) | copy-start | bytes 294916
  1.5 8.6 %collective-permute-start = (f32[4,1,8,128]{3,2,1,0:T(8,128)S(1)}, f32[4,1,8,128]{3,2,1,0:T(8,128)S(1)}, u32[]{:S(2)}, u32[]{:S(2)}) collective-permute-start(f32[4,1,8,128]{3,2,1,0:T(8,128)S(1)} %get-tuple-element.320), channel_id=1, source_target_pairs={{0,16},{16,32},{32,48},{48,64},{64,80},{80,96},{96,112},{112,128},... | collective-permute-start | bytes 49160 | tf_op jit(solution)/shard_map/ppermute | solution.py:15
  6.4 5.1 %collective-permute-start.1 = (f32[4,1,8,128]{3,2,1,0:T(8,128)S(1)}, f32[4,1,8,128]{3,2,1,0:T(8,128)S(1)}, u32[]{:S(2)}, u32[]{:S(2)}) collective-permute-start(f32[4,1,8,128]{3,2,1,0:T(8,128)S(1)} %get-tuple-element.321), channel_id=1, source_target_pairs={{16,0},{32,16},{48,32},{64,48},{80,64},{96,80},{112,96},{128,112},... | collective-permute-start | bytes 49160 | tf_op jit(solution)/shard_map/ppermute | solution.py:17
  12.8 7.3 %collective-permute-start.2 = (f32[4,26,1,128]{3,2,1,0:T(1,128)S(1)}, f32[4,26,1,128]{3,2,1,0:T(1,128)S(1)}, u32[]{:S(2)}, u32[]{:S(2)}) collective-permute-start(f32[4,26,1,128]{3,2,1,0:T(1,128)S(1)} %get-tuple-element.318), channel_id=1, source_target_pairs={{0,2},{2,4},{4,6},{6,8},{8,10},{10,12},{12,14},{1,3},{3,5},{5,7},{... | collective-permute-start | bytes 159752 | tf_op jit(solution)/shard_map/ppermute | solution.py:15
  16.0 4.9 %collective-permute-start.3 = (f32[4,26,1,128]{3,2,1,0:T(1,128)S(1)}, f32[4,26,1,128]{3,2,1,0:T(1,128)S(1)}, u32[]{:S(2)}, u32[]{:S(2)}) collective-permute-start(f32[4,26,1,128]{3,2,1,0:T(1,128)S(1)} %get-tuple-element.319), channel_id=1, source_target_pairs={{2,0},{4,2},{6,4},{8,6},{10,8},{12,10},{14,12},{3,1},{5,3},{7,5},{... | collective-permute-start | bytes 159752 | tf_op jit(solution)/shard_map/ppermute | solution.py:17
  21.7 8.4 %collective-permute-start.4 = (f32[4,26,10,1]{1,0,3,2:T(4,128)S(1)}, f32[4,26,10,1]{1,0,3,2:T(4,128)S(1)}, u32[]{:S(2)}, u32[]{:S(2)}) collective-permute-start(f32[4,26,10,1]{1,0,3,2:T(4,128)S(1)} %copy.118), channel_id=1, source_target_pairs={{0,1},{2,3},{4,5},{6,7},{8,9},{10,11},{12,13},{14,15},{16,17},{18,... | collective-permute-start | bytes 12488 | tf_op jit(solution)/shard_map/ppermute | solution.py:15
  23.4 7.3 %collective-permute-start.6 = (f32[4,26,10,1]{1,0,3,2:T(4,128)S(1)}, f32[4,26,10,1]{1,0,3,2:T(4,128)S(1)}, u32[]{:S(2)}, u32[]{:S(2)}) collective-permute-start(f32[4,26,10,1]{1,0,3,2:T(4,128)S(1)} %copy.126), channel_id=1, source_target_pairs={{1,0},{3,2},{5,4},{7,6},{9,8},{11,10},{13,12},{15,14},{17,16},{19,... | collective-permute-start | bytes 12488 | tf_op jit(solution)/shard_map/ppermute | solution.py:17
  30.7 1.8 copy-start.5
  32.5 1.3 copy-start.6
  34.4 4.8 %collective-permute-start.5 = (f32[3,8,128]{2,1,0:T(8,128)S(1)}, f32[3,8,128]{2,1,0:T(8,128)S(1)}, u32[]{:S(2)}, u32[]{:S(2)}) collective-permute-start(f32[3,8,128]{2,1,0:T(8,128)S(1)} %get-tuple-element.267), channel_id=1, source_target_pairs={{0,16},{16,32},{32,48},{48,64},{64,80},{80,96},{96,112},{112,128},... | collective-permute-start | bytes 36872 | tf_op jit(solution)/shard_map/ppermute | solution.py:27
  195.8 127.6 %copy-start.7 = (f32[24,8,128]{2,1,0:T(8,128)S(1)}, f32[24,8,128]{2,1,0:T(8,128)}, u32[]{:S(2)}) copy-start(f32[24,8,128]{2,1,0:T(8,128)} %param.11) | copy-start | bytes 294916
  195.9 128.2 %copy-start.4 = (f32[24,8,128]{2,1,0:T(8,128)}, f32[24,8,128]{2,1,0:T(8,128)S(1)}, u32[]{:S(2)}) copy-start(f32[24,8,128]{2,1,0:T(8,128)S(1)} %multiply_add_fusion.1) | copy-start | bytes 294916
  195.9 3.7 %collective-permute-start.7 = (f32[1,8,128]{2,1,0:T(8,128)S(1)}, f32[1,8,128]{2,1,0:T(8,128)S(1)}, u32[]{:S(2)}, u32[]{:S(2)}) collective-permute-start(f32[1,8,128]{2,1,0:T(8,128)S(1)} %get-tuple-element.335), channel_id=1, source_target_pairs={{0,16},{16,32},{32,48},{48,64},{64,80},{80,96},{96,112},{112,128},... | collective-permute-start | bytes 12296 | tf_op jit(solution)/shard_map/ppermute | solution.py:15
  198.3 4.4 %collective-permute-start.8 = (f32[1,8,128]{2,1,0:T(8,128)S(1)}, f32[1,8,128]{2,1,0:T(8,128)S(1)}, u32[]{:S(2)}, u32[]{:S(2)}) collective-permute-start(f32[1,8,128]{2,1,0:T(8,128)S(1)} %get-tuple-element.334), channel_id=1, source_target_pairs={{16,0},{32,16},{48,32},{64,48},{80,64},{96,80},{112,96},{128,112},... | collective-permute-start | bytes 12296 | tf_op jit(solution)/shard_map/ppermute | solution.py:17
  202.7 4.1 %collective-permute-start.10 = (f32[26,1,128]{2,1,0:T(1,128)S(1)}, f32[26,1,128]{2,1,0:T(1,128)S(1)}, u32[]{:S(2)}, u32[]{:S(2)}) collective-permute-start(f32[26,1,128]{2,1,0:T(1,128)S(1)} %get-tuple-element.332), channel_id=1, source_target_pairs={{0,2},{2,4},{4,6},{6,8},{8,10},{10,12},{12,14},{1,3},{3,5},{5,7},{... | collective-permute-start | bytes 39944 | tf_op jit(solution)/shard_map/ppermute | solution.py:15
  205.4 4.8 %collective-permute-start.9 = (f32[26,1,128]{2,1,0:T(1,128)S(1)}, f32[26,1,128]{2,1,0:T(1,128)S(1)}, u32[]{:S(2)}, u32[]{:S(2)}) collective-permute-start(f32[26,1,128]{2,1,0:T(1,128)S(1)} %get-tuple-element.333), channel_id=1, source_target_pairs={{2,0},{4,2},{6,4},{8,6},{10,8},{12,10},{14,12},{3,1},{5,3},{7,5},{... | collective-permute-start | bytes 39944 | tf_op jit(solution)/shard_map/ppermute | solution.py:17
  210.4 6.8 %collective-permute-start.11 = (f32[26,10,1]{2,1,0:T(8,128)S(1)}, f32[26,10,1]{2,1,0:T(8,128)S(1)}, u32[]{:S(2)}, u32[]{:S(2)}) collective-permute-start(f32[26,10,1]{2,1,0:T(8,128)S(1)} %get-tuple-element.324), channel_id=1, source_target_pairs={{1,0},{3,2},{5,4},{7,6},{9,8},{11,10},{13,12},{15,14},{17,16},{19,... | collective-permute-start | bytes 3128 | tf_op jit(solution)/shard_map/ppermute | solution.py:17
  215.8 3.4 %collective-permute-start.12 = (f32[26,10,1]{2,1,0:T(8,128)S(1)}, f32[26,10,1]{2,1,0:T(8,128)S(1)}, u32[]{:S(2)}, u32[]{:S(2)}) collective-permute-start(f32[26,10,1]{2,1,0:T(8,128)S(1)} %get-tuple-element.325), channel_id=1, source_target_pairs={{0,1},{2,3},{4,5},{6,7},{8,9},{10,11},{12,13},{14,15},{16,17},{18,... | collective-permute-start | bytes 3128 | tf_op jit(solution)/shard_map/ppermute | solution.py:15
where the time goes:
time: 325 us; the launch traced here: 324 us
  blocking collectives  254 us (78%)
  starting transfers between devices  35.5 us (11%)
  other arithmetic  15.1 us (5%)
  waiting for transfers between devices  11.2 us (3%)
  between operations  3.94 us (1%)
  local copies, waits for them, and re-layouts  3.32 us (1%)
    psum x1, blocking collectives, body(): lax.psum((jnp.sum(precond * image_old), jnp.sum(direction_in * image_old)...  108 us
    psum x1, blocking collectives, body(): lax.psum((jnp.sum(residual_in * direction_out), jnp.sum(direction_out * i...  101 us
    all_gather x1, blocking collectives, body(): lax.all_gather(jnp.stack([lower_coef, main_coef, upper_coef, source_coef]...  44 us
    ppermute x6, starting transfers between devices, with_halo(): lax.ppermute(head, axis, [((i + 1) % count, i) for i in range(ends)])  15.8 us
    ppermute x6, starting transfers between devices, with_halo(): lax.ppermute(tail, axis, [(i, (i + 1) % count) for i in range(ends)])  15.7 us
    ppermute x6, waiting for transfers between devices, with_halo(): lax.ppermute(head, axis, [((i + 1) % count, i) for i in range(ends)])  8.64 us
  transfers between devices with their start and end apart: 13, of which 6 were waited for; matrix products, arithmetic and copies ran while one was open for 2% of the time, Pallas kernels for 0%

commit v1 on v0

v1 whole, which is shorter than its diff:
```python
import jax
import jax.numpy as jnp
from jax import lax
from jax.experimental import pallas as pl
from jax.experimental.pallas import tpu as pltpu
from jax.sharding import PartitionSpec as P

PARTS = 3
QUARTERS = 4
WIDTH = 128 // QUARTERS
ROWS = 8
BACK = 2
LEFT = 2 * WIDTH
FLUX = LEFT + 1
SUMS = FLUX + WIDTH
VMEM = pl.BlockSpec(memory_space=pltpu.VMEM)
ANY = pl.BlockSpec(memory_space=pl.ANY)


def shape(*dims):
    return jax.ShapeDtypeStruct(dims, jnp.float32)


def shifted(value, axis, by):
    count = lax.axis_size(axis)
    return lax.ppermute(value, axis, [(i, i + by) for i in range(count) if 0 <= i + by < count])


def iota(axis):
    return lax.broadcasted_iota(jnp.int32, (8, 128), axis)


def down(tile, by=1):
    return pltpu.roll(tile, by % 8, 0)


def right(tile, by=1):
    return pltpu.roll(tile, by % 128, 1)


def lane(tile, at):
    return jnp.broadcast_to(tile[:, at:at + 1], (8, 128))


def far(y_got, k, v):
    return lane(y_got[k // 16], k % 16 * 8 + v)


def from_below(up, k, v, to=0):
    at = k * 5 + v
    return down(up[at // 8], to - at % 8)


def partial_diagonal(k, edge, cond_x, cond_y, cond_z, helmholtz):
    row, col = iota(0), iota(1)
    cx, cy = cond_x[k], cond_y[k]
    low_y = jnp.where(col == 0, edge, right(cy))
    low_x = jnp.where(row == 0, 0.0, down(cx))
    total = helmholtz[k] + cx + low_x + cy + low_y + cond_z[k]
    return total + cond_z[k - 1] if k else total


def face_kernel(*refs):
    given, y_face, x_face, held, sems = refs[:6], refs[6], refs[7], refs[8:14], refs[14]
    n = given[0].shape[0]
    copies = [pltpu.make_async_copy(src, dst, sems.at[a]) for a, (src, dst) in enumerate(zip(given, held))]
    for copy in copies:
        copy.start()
    for copy in copies:
        copy.wait()
    dirn, resid, cond_x, cond_y, cond_z, helmholtz = held
    row, col = iota(0), iota(1)
    face = 127 - 127 * lax.axis_index("gy")
    y_tiles = [jnp.zeros((8, 128), jnp.float32) for t in range(y_face.shape[0])]
    x_tiles = [jnp.zeros((8, 128), jnp.float32) for t in range(x_face.shape[0])]
    for k in range(n):
        diag = partial_diagonal(k, 0.0, cond_x, cond_y, cond_z, helmholtz)
        for v, value in enumerate((dirn[k], cond_y[k], diag, cond_z[k], resid[k], cond_x[k])):
            at = k % 16 * 8 + v
            moved = pltpu.roll(value, lax.rem(at - face + 256, 128), 1)
            y_tiles[k // 16] = jnp.where(col == at, moved, y_tiles[k // 16])
        for v, value in enumerate((dirn[k], cond_x[k], diag, cond_z[k], resid[k])):
            at = k * 5 + v
            x_tiles[at // 8] = jnp.where(row == at % 8, down(value, at % 8 - 7), x_tiles[at // 8])
    for ref, tiles in ((y_face, y_tiles), (x_face, x_tiles)):
        for t, tile in enumerate(tiles):
            ref[t] = tile


def condense(main, link, source):
    n = len(main)
    zero = jnp.zeros_like(main[0])
    base, first, last = [zero] * n, [zero + 1.0] + [zero] * (n - 1), [zero] * n
    for k in range(1, n):
        low = link[k - 1]
        inv = 1.0 / (main[k] - low * last[k - 1] if k > 1 else main[k])
        base[k] = (source[k] + low * base[k - 1]) * inv if k > 1 else source[k] * inv
        first[k] = low * first[k - 1] * inv
        last[k] = link[k] * inv
    for k in range(n - 2, 0, -1):
        ratio = last[k]
        base[k] = base[k] + ratio * base[k + 1]
        first[k] = first[k] + ratio * first[k + 1]
        last[k] = ratio * last[k + 1]
    return base, first, last


def ends(main, link, source, parts):
    base, first, last = parts
    return [
        main[0] - link[0] * first[1],
        link[0] * last[1],
        source[0] + link[0] * base[1],
        link[-1] - link[-1] * last[-1],
        link[-1] * base[-1],
    ]


def sides(core, field, below, beside):
    row, col = iota(0), iota(1)
    after = jnp.where(row == 7, 0.0, down(field, -1))
    before = jnp.where(row == 0, below, down(field))
    upper = jnp.where(col == 127, jnp.where(core == 0, beside, 0.0), right(field, -1))
    lower = jnp.where(col == 0, jnp.where(core == 0, 0.0, beside), right(field))
    return after, before, upper, lower


def block_kernel(dirn, resid, cond_x, cond_y, cond_z, helmholtz, y_got, diagonal_got, up,
                 spread, own_parts, ext_parts, far_parts, image, lows):
    core = lax.axis_index("gy")
    row, col = iota(0), iota(1)
    n = dirn.shape[0]
    levels = range(n)
    first_row = lambda a: jnp.where(row == 0, a, 0.0)

    own_m, ext_m, far_m, ext_c, ext_r, far_c, far_r = [], [], [], [], [], [], []
    low_xs, low_ys, sides_d, ext_ds = [], [], [], []
    for k in levels:
        cx, cy = cond_x[k], cond_y[k]
        low_x = jnp.where(row == 0, from_below(up, k, 1), down(cx))
        edge = jnp.where(core == 1, far(y_got, k, 1), 0.0)
        low_y = jnp.where(col == 0, edge, right(cy))
        diag = partial_diagonal(k, edge, cond_x, cond_y, cond_z, helmholtz)
        low_xs.append(low_x)
        low_ys.append(low_y)
        own_m.append(diag + first_row(low_x))
        corner = jnp.where(jnp.logical_and(core == 1, col == 0), down(far(diagonal_got, k, 1), 1), 0.0)
        found = first_row(from_below(up, k, 2) + corner)
        ext_m.append(jnp.where(found > 0.0, found, 1.0))
        ext_c.append(first_row(from_below(up, k, 3)))
        ext_r.append(first_row(from_below(up, k, 4)))
        far_m.append(far(y_got, k, 2) + first_row(down(far(diagonal_got, k, 5), 1))
                     + jnp.where(core == 0, lane(cy, 127), 0.0))
        far_c.append(far(y_got, k, 3))
        far_r.append(far(y_got, k, 4))
        ext_ds.append(first_row(from_below(up, k, 0)))
        after, before, upper, lower = sides(core, dirn[k], ext_ds[k], far(y_got, k, 0))
        sides_d.append(cx * after + low_x * before + cy * upper + low_y * lower)
        lows[0, k] = low_x
        lows[1, k] = low_y

    own_c = [cond_z[k] for k in levels]
    own_r = [resid[k] for k in levels]
    own = condense(own_m, own_c, own_r)
    ext = condense(ext_m, ext_c, ext_r)
    beside = condense(far_m, far_c, far_r)
    for ref, parts in ((own_parts, own), (ext_parts, ext), (far_parts, beside)):
        for v in range(3):
            for k in levels:
                ref[v, k] = parts[v][k]

    zero = jnp.zeros((8, 128), jnp.float32)
    c0 = g0 = g1 = g2 = h0 = h1 = h2 = d_ad = r_d = zero
    below_g1 = below_g2 = below_h1 = below_h2 = zero
    quad_x, quad_y = [zero] * 4, [zero] * 4
    flux = zero
    for k in levels:
        d, cx, cy = dirn[k], cond_x[k], cond_y[k]
        low_x, low_y, side = low_xs[k], low_ys[k], sides_d[k]
        b, f, l = own[0][k], own[1][k], own[2][k]
        eb, ef, el = ext[0][k], ext[1][k], ext[2][k]
        face_d, face_b = first_row(low_x * d), first_row(low_x * b)
        below_g1 = below_g1 + face_d * ef
        below_g2 = below_g2 + face_d * el
        g0 = g0 + face_d * eb
        if k:
            after, before, upper, lower = sides(core, b, eb, beside[0][k])
            side_b = cx * after + low_x * before + cy * upper + low_y * lower
            c0 = c0 + resid[k] * b
            g0 = g0 + side * b
            h0 = h0 + side_b * b + face_b * eb
            h1 = h1 + side_b * f
            h2 = h2 + side_b * l
            g2 = g2 + side * l
            below_h1 = below_h1 + face_b * ef
            below_h2 = below_h2 + face_b * el
        g1 = g1 + side * f
        fx = jnp.where(row == 0, ef, down(f))
        lx = jnp.where(row == 0, el, down(l))
        fy = jnp.where(col == 0, beside[1][k], right(f))
        ly = jnp.where(col == 0, beside[2][k], right(l))
        for quad, cond, f_to, l_to in ((quad_x, low_x, fx, lx), (quad_y, low_y, fy, ly)):
            cf, cl = cond * f, cond * l
            for at, term in enumerate((cf * f_to, cf * l_to, cl * f_to, cl * l_to)):
                quad[at] = quad[at] + term
        local = (helmholtz[k] + cx + low_x + cy + low_y) * d - side
        d_ad = d_ad + d * local - face_d * ext_ds[k]
        r_d = r_d + resid[k] * d
        local = local - flux
        if k + 1 < n:
            gap = d - dirn[k + 1]
            flux = cond_z[k] * gap
            d_ad = d_ad + flux * gap
            local = local + flux
        image[k] = local

    chain = ends(own_m, own_c, own_r, own)
    chain_ext = ends(ext_m, ext_c, ext_r, ext)
    chain_far = ends(far_m, far_c, far_r, beside)
    chain_x = [jnp.where(row == 0, e, down(o)) for o, e in zip(chain, chain_ext)]
    chain_y = [jnp.where(col == 0, e, right(o)) for o, e in zip(chain, chain_far)]
    spot = lax.rem(col, WIDTH)
    left = sums = zero
    for v in range(5):
        left = jnp.where(spot == v, right(chain_y[v], v), left)
    for v, part in enumerate((c0, g0, h0, d_ad, r_d)):
        sums = jnp.where(col == v, jnp.sum(part, axis=1, keepdims=True), sums)
    others = ([2.0 * q for q in quad_x] + [2.0 * q for q in quad_y]
              + [2.0 * h1, 2.0 * h2, g1, g2, 2.0 * below_h1, 2.0 * below_h2, below_g1, below_g2]
              + [dirn[0], dirn[n - 1], cond_z[n - 1], left, sums, zero])
    table = [[chain[v], chain_x[v], others[2 * v], others[2 * v + 1]] for v in range(5)]
    table += [others[at:at + 4] for at in (10, 14, 18)]
    block = lax.div(col, WIDTH)
    for quarter in range(QUARTERS):
        for at, values in enumerate(table):
            tile = zero
            for b, value in enumerate(values):
                tile = jnp.where(block == b, right(value, WIDTH * (b - quarter)), tile)
            spread[pl.ds(quarter * ROWS + at, 8, stride=QUARTERS * ROWS), :] = tile


def row_kernel(back, own_parts, dirn, low):
    row = iota(0)
    tiles = [jnp.zeros((8, 128), jnp.float32) for t in range(low.shape[0])]
    for k in range(dirn.shape[0]):
        for v, value in enumerate((own_parts[0, k], own_parts[1, k], own_parts[2, k], dirn[k])):
            at = k * 4 + v
            tiles[at // 8] = jnp.where(row == at % 8, down(value, at % 8), tiles[at // 8])
    for t, tile in enumerate(tiles):
        low[t] = tile


def solver_kernel(rows, back, mains, links, sources, found):
    n = rows.shape[0] // ROWS
    half = n // 2
    lanes = lax.broadcasted_iota(jnp.int32, (n, 128), 1)
    level = lax.broadcasted_iota(jnp.int32, (n, 128), 0)
    take = lambda at: rows[pl.ds(at, n, stride=ROWS), :]
    shift_to = lambda value, by: pltpu.roll(value, by % 128, 1)
    previous = lambda value: jnp.where(level == 0, 0.0, pltpu.roll(value, 1, 0))
    lines = [take(at) for at in range(ROWS)]

    def other(v):
        at, b = (v // 2, 2 + v % 2) if v < 10 else (5 + (v - 10) // 4, (v - 10) % 4)
        return shift_to(lines[at], -b * WIDTH)

    left = other(19)
    chain = []
    for v in range(5):
        value = jnp.where(lanes == LEFT, shift_to(left, LEFT - v), lines[v])
        chain.append(jnp.where(lanes > LEFT, 1.0 if v == 0 else 0.0, value))
    source = chain[2] + previous(chain[4])
    mains[...] = chain[0] + previous(chain[3])
    links[...] = chain[1]
    sources[...] = source
    main = [mains[j:j + 1, :] for j in range(n)]
    link = [links[j:j + 1, :] for j in range(n)]
    src = [sources[j:j + 1, :] for j in range(n)]
    ratio, shift = [None] * n, [None] * n
    for j in range(half):
        a, b = j, n - 1 - j
        if j:
            inv_a = 1.0 / (main[a] - link[a - 1] * ratio[a - 1])
            inv_b = 1.0 / (main[b] - link[b] * ratio[b + 1])
            shift[a] = (src[a] + link[a - 1] * shift[a - 1]) * inv_a
            shift[b] = (src[b] + link[b] * shift[b + 1]) * inv_b
        else:
            inv_a, inv_b = 1.0 / main[a], 1.0 / main[b]
            shift[a], shift[b] = src[a] * inv_a, src[b] * inv_b
        ratio[a] = link[a] * inv_a
        ratio[b] = link[b - 1] * inv_b
    x = [None] * n
    a, b = half - 1, half
    x[a] = (shift[a] + ratio[a] * shift[b]) / (1.0 - ratio[a] * ratio[b])
    x[b] = shift[b] + ratio[b] * x[a]
    for j in range(half - 2, -1, -1):
        x[j] = shift[j] + ratio[j] * x[j + 1]
        m = n - 1 - j
        x[m] = shift[m] + ratio[m] * x[m - 1]
    for j in range(n):
        found[j:j + 1, :] = x[j]

    x = found[...]
    x2 = jnp.where(level == n - 1, 0.0, pltpu.roll(x, n - 1, 0))
    below, below2 = shift_to(x, -WIDTH), shift_to(x2, -WIDTH)
    beside = jnp.where(lanes == 0, shift_to(x, -LEFT), shift_to(x, 1))
    beside2 = jnp.where(lanes == 0, shift_to(x2, -LEFT), shift_to(x2, 1))
    quad = (x * (other(0) * below + other(1) * below2 + other(4) * beside + other(5) * beside2)
            + x2 * (other(2) * below + other(3) * below2 + other(6) * beside + other(7) * beside2))
    sum_h = quad + x * other(8) + x2 * other(9) + below * other(12) + below2 * other(13)
    sum_g = x * other(10) + x2 * other(11) + below * other(14) + below2 * other(15)
    gap = other(17) - jnp.where(level == n - 1, 0.0, pltpu.roll(other(16), n - 1, 0))
    flux = other(18) * gap
    amounts = [x * source, sum_g, sum_h, flux * gap, None]
    known = jnp.sum(other(20), axis=0, keepdims=True)
    lane_row = lax.broadcasted_iota(jnp.int32, (1, 128), 1)
    scalars = jnp.where(lane_row < 5, known, 0.0)
    for v, amount in enumerate(amounts[:4]):
        amount = jnp.where(lane_row < WIDTH, jnp.sum(amount, axis=0, keepdims=True), 0.0)
        scalars = scalars + jnp.where(lane_row == v, jnp.sum(amount, axis=1, keepdims=True), 0.0)
    scalars = jnp.broadcast_to(pltpu.roll(jnp.broadcast_to(scalars, (8, 128)), SUMS, 1)[0:1, :], (n, 128))
    in_flux = jnp.logical_and(lanes >= FLUX, lanes < SUMS)
    tail = jnp.where(lanes >= SUMS, scalars, 0.0)
    back[pl.ds(0, n, stride=BACK), :] = jnp.where(
        lanes <= LEFT, x, jnp.where(in_flux, shift_to(previous(flux), FLUX), tail))
    back[pl.ds(1, n, stride=BACK), :] = jnp.where(lanes <= LEFT, x2, jnp.where(in_flux, shift_to(flux, FLUX), tail))


def scalar_kernel(tops, got, spread):
    n = got.shape[0] // BACK
    amount = jnp.sum(got[pl.ds(0, n, stride=BACK), :], axis=0, keepdims=True)
    for t in range(0, spread.shape[0], 3):
        spread[t] = amount
        spread[t + 1] = tops[0:1, :]
        spread[t + 2] = tops[1:2, :]


def column_kernel(low, got, resid, cond_x, cond_y, own_parts, ext_parts, far_parts, image_in, lows,
                  precond, image_p, image_d, tops):
    core = lax.axis_index("gy")
    n = resid.shape[0]
    block = lax.div(iota(1), WIDTH)
    part = lambda quarter, v: got[pl.ds(quarter * BACK + v, 8, stride=QUARTERS * BACK), :]

    def gather(v, lane_from):
        tile = jnp.zeros((8, 128), jnp.float32)
        for quarter in range(QUARTERS):
            tile = jnp.where(block == quarter, right(part(quarter, v), WIDTH * quarter - lane_from), tile)
        return tile

    x, x2 = gather(0, 0), gather(1, 0)
    ext_x, ext_x2 = gather(0, WIDTH), gather(1, WIDTH)
    far_x, far_x2 = lane(part(0, 0), LEFT), lane(part(0, 1), LEFT)
    flux_below, flux_above = gather(0, FLUX), gather(1, FLUX)
    tops[...] = jnp.where(iota(0) == 0, x, down(x2))
    join = lambda parts, k, a, b: parts[0, k] + a * parts[1, k] + b * parts[2, k]
    for k in range(n):
        p = join(own_parts, k, x, x2)
        ext = join(ext_parts, k, ext_x, ext_x2)
        beside = join(far_parts, k, far_x, far_x2)
        after, before, upper, lower = sides(core, p, ext, beside)
        side = cond_x[k] * after + lows[0, k] * before + cond_y[k] * upper + lows[1, k] * lower
        precond[k] = p
        image_p[k] = resid[k] - side
        local = image_in[k]
        if k == 0:
            local = local - flux_below
        if k == n - 1:
            local = local + flux_above
        image_d[k] = local


def update_kernel(scalars, low, cond_x, sol, resid, dirn, precond, image_p, image_d,
                  sol_to, res_to, dir_to, sol_out, res_out, dir_out, sems):
    row = iota(0)
    mates = scalars.shape[0] // 3
    amount = scalars[0]
    for t in range(1, mates):
        amount = amount + scalars[3 * t]
    per_row = lax.axis_size("gy")
    mate = lax.axis_index("gx") * per_row + lax.axis_index("gy") + per_row
    mate = jnp.minimum(mate, mates - 1)
    x, x2 = (jnp.broadcast_to(scalars[3 * mate + v], (8, 128)) for v in (1, 2))
    r_p, p_nd, p_np, d_ad, r_d = (jnp.broadcast_to(amount[:, v:v + 1], (8, 128)) for v in range(SUMS, SUMS + 5))
    p_ad = r_d - p_nd
    conj = -p_ad / d_ad
    step = (r_p + conj * r_d) / (r_p - p_np + conj * p_ad)
    n = sol.shape[0]
    size = n // PARTS
    copies = []
    for k in range(n):
        out = precond[k] + conj * dirn[k]
        dir_out[k] = out
        sol_out[k] = sol[k] + step * out
        b_up, f_up, l_up, d_up = (down(low[(4 * k + v) // 8], 7 - (4 * k + v) % 8) for v in range(4))
        p_up = b_up + x * f_up + x2 * l_up
        above = jnp.where(row == 7, cond_x[k] * (p_up + conj * d_up), 0.0)
        res_out[k] = resid[k] - step * (image_p[k] + conj * image_d[k] - above)
        if (k + 1) % size == 0:
            part = k // size
            levels = pl.ds(part * size, size)
            for a, (src, dst) in enumerate(((sol_out, sol_to), (res_out, res_to), (dir_out, dir_to))):
                copies.append(pltpu.make_async_copy(src.at[levels], dst.at[levels], sems.at[3 * part + a]))
                copies[-1].start()
    for copy in copies:
        copy.wait()


def call(kernel, outs, *args, scratch=(), first=0, out_spec=VMEM):
    many = isinstance(outs, tuple)
    return pl.pallas_call(
        kernel, out_shape=outs, in_specs=[ANY] * first + [VMEM] * (len(args) - first),
        out_specs=(out_spec,) * len(outs) if many else out_spec, scratch_shapes=scratch,
        compiler_params=pltpu.CompilerParams(vmem_limit_bytes=8 << 20))(*args)


def body(solution_in, residual_in, direction_in, cond_x, cond_y, cond_z, helmholtz):
    nz, nx, ny = direction_in.shape
    gz, gx = lax.axis_size("gz"), lax.axis_size("gx")
    mates = gx * lax.axis_size("gy")
    field = shape(nz, nx, ny)
    parts = shape(3, nz, nx, ny)
    given = [pltpu.with_memory_space_constraint(a, pltpu.HBM)
             for a in (direction_in, residual_in, cond_x, cond_y, cond_z, helmholtz)]

    y_face, x_face, *given = call(
        face_kernel, (shape(-(-nz // 16), nx, ny), shape(nz * 5 // 8, nx, ny)) + (field,) * 6, *given,
        scratch=(pltpu.SemaphoreType.DMA((6,)),), first=6)
    direction_in, residual_in, cond_x, cond_y, cond_z, helmholtz = given
    up = shifted(x_face, "gx", 1)
    y_got = lax.ppermute(y_face, "gy", [(0, 1), (1, 0)])
    diagonal_got = lax.ppermute(y_face, ("gx", "gy"), [
        (2 * i + c, 2 * i + 3 - c) for i in range(gx - 1) for c in range(2)])
    spread, own_parts, ext_parts, far_parts, image, lows = call(
        block_kernel, (shape(gz * ROWS, ny), parts, parts, parts, field, shape(2, nz, nx, ny)),
        *given, y_got, diagonal_got, up)
    rows = lax.all_to_all(spread.reshape(gz, ROWS, ny), "gz", 0, 0, tiled=True)
    back = call(solver_kernel, shape(gz * BACK, ny), rows.reshape(gz * ROWS, ny),
                scratch=(pltpu.VMEM((gz, ny), jnp.float32),) * 4)
    low = call(row_kernel, shape(nz // 2, nx, ny), back, own_parts, direction_in, first=1)
    low = shifted(low, "gx", -1)
    got = lax.all_to_all(back.reshape(gz, BACK, ny), "gz", 0, 0, tiled=True).reshape(gz * BACK, ny)
    precond, image_p, image_d, tops = call(
        column_kernel, (field, field, field, shape(8, ny)), low, got, residual_in, cond_x, cond_y,
        own_parts, ext_parts, far_parts, image, lows, first=1)
    sums = call(scalar_kernel, shape(mates * 3, 1, ny), tops, got)
    sums = lax.all_to_all(sums, ("gx", "gy"), 0, 0, tiled=True)
    return call(update_kernel, (field, field, field), sums, low, cond_x, solution_in, residual_in, direction_in,
                precond, image_p, image_d, out_spec=ANY,
                scratch=(pltpu.VMEM((nz, nx, ny), jnp.float32),) * 3 + (pltpu.SemaphoreType.DMA((3 * PARTS,)),))


def solution(mesh):
    spec = P("gz", "gx", "gy")
    return jax.shard_map(body, mesh=mesh, in_specs=(spec,) * 7, out_specs=(spec,) * 3, check_vma=False)
```

time: 325 us -> 67.7 us (0.21)
  blocking collectives: 254 us -> 36.2 us
  starting transfers between devices: 35.5 us -> 17.1 us
  other arithmetic: 15.1 us -> 0 us
  Pallas kernels: 0 us -> 5.02 us
  local copies, waits for them, and re-layouts: 3.32 us -> 0.01 us
    psum x2 -> x0, blocking collectives: 210 us -> none  [the longest x1 108 us: body(): lax.psum((jnp.sum(precond * image_old), jnp.sum(direction_in * image_old)...]
    all_gather x1 -> x0, blocking collectives: 44 us -> none  [body(): lax.all_gather(jnp.stack([lower_coef, main_coef, upper_coef, source_coef]...]
    all_to_all x0 -> x2, blocking collectives: none -> 36.2 us  [the longest x1 20.8 us: body(): rows = lax.all_to_all(spread.reshape(gz, ROWS, ny), 'gz', 0, 0, tiled=True)]
    ppermute x13 -> x4, starting transfers between devices: 35.5 us -> 12.7 us  [the longest x2 5.33 us: shifted(): lax.ppermute(value, axis, [(i, i + by) for i in range(count) if 0 <= i +...]
    ppermute x13 -> x4, waiting for transfers between devices: 11.2 us -> 4.63 us  [the longest x2 3.83 us: shifted(): lax.ppermute(value, axis, [(i, i + by) for i in range(count) if 0 <= i +...]
    pallas_call x0 -> x7, Pallas kernels: none -> 5.02 us  [call(): pl.pallas_call(kernel, out_shape=outs, in_specs=[ANY] * first + [VMEM] *...]
    all_to_all x0 -> x1, starting transfers between devices: none -> 4.43 us  [body(): lax.all_to_all(back.reshape(gz, BACK, ny), 'gz', 0, 0, tiled=True)]
    another operation x3 -> x0, other arithmetic: 4.33 us -> none  [the longest x2 4.32 us: body(): stacked = jnp.stack([direction_in, cond_x, cond_y, cond_z])]
  transfers between devices with their start and end apart: 13 -> 5, of which waited for: 6 -> 3; matrix products, arithmetic and copies ran while one was open for 2% -> 0% of each run, Pallas kernels for 0% -> 0%
where the time goes in v1:
time: 67.7 us; the launch traced here: 67.3 us
  blocking collectives  36.2 us (53%)
  starting transfers between devices  17.1 us (25%)
  waiting for transfers between devices  8.23 us (12%)
  Pallas kernels  5.02 us (7%)
  between operations  0.73 us (1%)
    all_to_all x1, blocking collectives, body(): rows = lax.all_to_all(spread.reshape(gz, ROWS, ny), 'gz', 0, 0, tiled=True)  20.8 us
    all_to_all x1, blocking collectives, body(): sums = lax.all_to_all(sums, ('gx', 'gy'), 0, 0, tiled=True)  15.4 us
    ppermute x2, starting transfers between devices, shifted(): lax.ppermute(value, axis, [(i, i + by) for i in range(count) if 0 <= i +...  5.33 us
    pallas_call x7, Pallas kernels, call(): pl.pallas_call(kernel, out_shape=outs, in_specs=[ANY] * first + [VMEM] *...  5.02 us
    all_to_all x1, starting transfers between devices, body(): lax.all_to_all(back.reshape(gz, BACK, ny), 'gz', 0, 0, tiled=True)  4.43 us
    ppermute x1, starting transfers between devices, body(): lax.ppermute(y_face, ('gx', 'gy'), [(2 * i + c, 2 * i + 3 - c) for i in r...  4.04 us
    ppermute x2, waiting for transfers between devices, shifted(): lax.ppermute(value, axis, [(i, i + by) for i in range(count) if 0 <= i +...  3.83 us
    all_to_all x1, waiting for transfers between devices, body(): lax.all_to_all(back.reshape(gz, BACK, ny), 'gz', 0, 0, tiled=True)  3.6 us
  transfers between devices with their start and end apart: 5, of which 3 were waited for; matrix products, arithmetic and copies ran while one was open for 0% of the time, Pallas kernels for 0%

profile of v1, /device:TPU:1, one launch (start us, length us, event | category | flops | bytes accessed | tf_op | source)
XLA Modules:
  0.0 67.3 jit_solution(1534511624706546266)
XLA Ops:
  0.6 1.7 %shard_map.94 = (f32[2,8,128]{2,1,0:T(8,128)S(1)}, f32[15,8,128]{2,1,0:T(8,128)S(1)}, f32[24,8,128]{2,1,0:T(8,128)S(1)}, f32[24,8,128]{2,1,0:T(8,128)S(1)}, f32[...) custom-call(f32[24,8,128]{2,1,0:T(8,128)} %refs_0_.1, ...), custom_call_target="tpu_custom_call" | custom-call | tf_op jit(solution)/shard_map/pallas_call | solution.py:411
  2.3 4.0 %collective-permute-start.2 = (f32[15,8,128]{2,1,0:T(8,128)S(1)}, f32[15,8,128]{2,1,0:T(8,128)S(1)}, u32[]{:S(2)}, u32[]{:S(2)}) collective-permute-start(f32[15,8,128]{2,1,0:T(8,128)S(1)} %get-tuple-element.28), channel_id=1, source_target_pairs={{0,2},{2,4},{4,6},{6,8},{8,10},{10,12},{12,14},{1,3},{3,5},{5,7},{... | collective-permute-start | bytes 184328 | tf_op jit(solution)/shard_map/ppermute | solution.py:26
  6.3 4.0 %collective-permute-start.1 = (f32[2,8,128]{2,1,0:T(8,128)S(1)}, f32[2,8,128]{2,1,0:T(8,128)S(1)}, u32[]{:S(2)}, u32[]{:S(2)}) collective-permute-start(f32[2,8,128]{2,1,0:T(8,128)S(1)} %get-tuple-element.27), channel_id=1, source_target_pairs={{0,3},{1,2},{2,5},{3,4},{4,7},{5,6},{6,9},{7,8},{8,11},{9,10},{10,... | collective-permute-start | bytes 24584 | tf_op jit(solution)/shard_map/ppermute | solution.py:432
  10.4 3.3 %collective-permute-start = (f32[2,8,128]{2,1,0:T(8,128)S(1)}, f32[2,8,128]{2,1,0:T(8,128)S(1)}, u32[]{:S(2)}, u32[]{:S(2)}) collective-permute-start(f32[2,8,128]{2,1,0:T(8,128)S(1)} %get-tuple-element.27), channel_id=1, source_target_pairs={{0,1},{1,0},{2,3},{3,2},{4,5},{5,4},{6,7},{7,6},{8,9},{9,8},{10,11... | collective-permute-start | bytes 24584 | tf_op jit(solution)/shard_map/ppermute | solution.py:431
  13.7 0.0 collective-permute-done.1.diagonal_got
  13.7 0.8 %collective-permute-done.y_got = f32[2,8,128]{2,1,0:T(8,128)S(1)} collective-permute-done((f32[2,8,128]{2,1,0:T(8,128)S(1)}, f32[2,8,128]{2,1,0:T(8,128)S(1)}, u32[]{:S(2)}, u32[]{:S(2)}) %collective-permute-start) | collective-permute-done | bytes 8224 | tf_op jit(solution)/shard_map/ppermute | solution.py:431
  14.5 0.0 collective-permute-done.2.up
  14.5 1.0 %shard_map.95 = (f32[256,128]{1,0:T(8,128)S(1)}, f32[3,24,8,128]{3,2,1,0:T(8,128)S(1)}, f32[3,24,8,128]{3,2,1,0:T(8,128)S(1)}, f32[3,24,8,128]{3,2,1,0:T(8,128)S...) custom-call(f32[24,8,128]{2,1,0:T(8,128)S(1)} %get-tuple-element.21.dirn, ...), custom_call_target="tpu_custom_call" | custom-call | tf_op jit(solution)/shard_map/pallas_call | solution.py:411
  15.5 20.8 %all_to_all.15 = f32[32,8,128]{2,1,0:T(8,128)S(1)} all-to-all(f32[32,8,128]{2,1,0:T(8,128)S(1)} %bitcast.7), channel_id=1, replica_groups=mesh['gz'=32,'gx'=8,'gy'=2] {'gz'}, dimensions={0} | all-to-all | bytes 262144 | tf_op jit(solution)/shard_map/all_to_all | solution.py:437
  36.3 1.2 %shard_map.96.back = f32[64,128]{1,0:T(8,128)} custom-call(f32[256,128]{1,0:T(8,128)S(1)} %bitcast.4), custom_call_target="tpu_custom_call" | custom-call | tf_op jit(solution)/shard_map/pallas_call | solution.py:411
  37.5 4.4 %all-to-all-start.1 = ((f32[32,2,128]{2,1,0:T(2,128)}), f32[32,2,128]{2,1,0:T(2,128)S(1)}, u32[]{:S(2)}, u32[]{:S(2)}) async-start(f32[32,2,128]{2,1,0:T(2,128)} %bitcast.2), calls=%async_computation.1 | async-start | bytes 65536 | tf_op jit(solution)/shard_map/all_to_all | solution.py:442
  42.0 1.3 %collective-permute-start.3 = (f32[12,8,128]{2,1,0:T(8,128)S(1)}, f32[12,8,128]{2,1,0:T(8,128)S(1)}, u32[]{:S(2)}, u32[]{:S(2)}) collective-permute-start(f32[12,8,128]{2,1,0:T(8,128)S(1)} %shard_map.97), channel_id=1, source_target_pairs={{2,0},{4,2},{6,4},{8,6},{10,8},{12,10},{14,12},{3,1},{5,3},{7,5},{... | collective-permute-start | bytes 147464 | tf_op jit(solution)/shard_map/ppermute | solution.py:26
  43.3 3.8 %collective-permute-done.3.low = f32[12,8,128]{2,1,0:T(8,128)S(1)} collective-permute-done((f32[12,8,128]{2,1,0:T(8,128)S(1)}, f32[12,8,128]{2,1,0:T(8,128)S(1)}, u32[]{:S(2)}, u32[]{:S(2)}) %collective-permute-start.3) | collective-permute-done | bytes 49184 | tf_op jit(solution)/shard_map/ppermute | solution.py:26
  47.1 3.6 %all-to-all-done.1 = f32[32,2,128]{2,1,0:T(2,128)S(1)} async-done(((f32[32,2,128]{2,1,0:T(2,128)}), f32[32,2,128]{2,1,0:T(2,128)S(1)}, u32[]{:S(2)}, u32[]{:S(2)}) %all-to-all-start.1) | async-done | bytes 32800 | tf_op jit(solution)/shard_map/all_to_all | solution.py:442
  50.7 0.2 shard_map.98
  50.9 0.0 copy-start
  51.0 15.4 %all_to_all.16.scalars = f32[48,1,128]{2,1,0:T(1,128)S(1)} all-to-all(f32[48,1,128]{2,1,0:T(1,128)S(1)} %shard_map.99), channel_id=1, replica_groups=mesh['gz'=32,'gx'=8,'gy'=2] {'gx','gy'}, dimensions={0} | all-to-all | bytes 49152 | tf_op jit(solution)/shard_map/all_to_all | solution.py:447
  66.4 0.0 copy-done
  66.4 0.9 %shard_map.100 = (f32[24,8,128]{2,1,0:T(8,128)}, f32[24,8,128]{2,1,0:T(8,128)}, f32[24,8,128]{2,1,0:T(8,128)}) custom-call(f32[48,1,128]{2,1,0:T(1,128)S(1)} %all_to_all.16.scalars, f32[12,8,128]{2,1,0:T(8,128)S(1)} %collective-permute-done.3.low, f32[24,8,128]{2,1,0:T(8,128)S(1)} %get-tuple-element.23.cond_x, f32[24,8,128]{2,1,0:T(8,128)S(1)} %copy-done, ...), custom_call_target="tpu_custom_call" | custom-call | tf_op jit(solution)/shard_map/pallas_call | solution.py:411
  (2 shorter events, 0.0 us)
Async XLA Ops:
  2.3 12.2 %collective-permute-start.2 = (f32[15,8,128]{2,1,0:T(8,128)S(1)}, f32[15,8,128]{2,1,0:T(8,128)S(1)}, u32[]{:S(2)}, u32[]{:S(2)}) collective-permute-start(f32[15,8,128]{2,1,0:T(8,128)S(1)} %get-tuple-element.28), channel_id=1, source_target_pairs={{0,2},{2,4},{4,6},{6,8},{8,10},{10,12},{12,14},{1,3},{3,5},{5,7},{... | collective-permute-start | bytes 184328 | tf_op jit(solution)/shard_map/ppermute | solution.py:26
  6.3 7.4 %collective-permute-start.1 = (f32[2,8,128]{2,1,0:T(8,128)S(1)}, f32[2,8,128]{2,1,0:T(8,128)S(1)}, u32[]{:S(2)}, u32[]{:S(2)}) collective-permute-start(f32[2,8,128]{2,1,0:T(8,128)S(1)} %get-tuple-element.27), channel_id=1, source_target_pairs={{0,3},{1,2},{2,5},{3,4},{4,7},{5,6},{6,9},{7,8},{8,11},{9,10},{10,... | collective-permute-start | bytes 24584 | tf_op jit(solution)/shard_map/ppermute | solution.py:432
  10.4 4.1 %collective-permute-start = (f32[2,8,128]{2,1,0:T(8,128)S(1)}, f32[2,8,128]{2,1,0:T(8,128)S(1)}, u32[]{:S(2)}, u32[]{:S(2)}) collective-permute-start(f32[2,8,128]{2,1,0:T(8,128)S(1)} %get-tuple-element.27), channel_id=1, source_target_pairs={{0,1},{1,0},{2,3},{3,2},{4,5},{5,4},{6,7},{7,6},{8,9},{9,8},{10,11... | collective-permute-start | bytes 24584 | tf_op jit(solution)/shard_map/ppermute | solution.py:431
  37.5 13.2 %all-to-all-start.1 = ((f32[32,2,128]{2,1,0:T(2,128)}), f32[32,2,128]{2,1,0:T(2,128)S(1)}, u32[]{:S(2)}, u32[]{:S(2)}) async-start(f32[32,2,128]{2,1,0:T(2,128)} %bitcast.2), calls=%async_computation.1 | async-start | bytes 65536 | tf_op jit(solution)/shard_map/all_to_all | solution.py:442
  42.0 5.1 %collective-permute-start.3 = (f32[12,8,128]{2,1,0:T(8,128)S(1)}, f32[12,8,128]{2,1,0:T(8,128)S(1)}, u32[]{:S(2)}, u32[]{:S(2)}) collective-permute-start(f32[12,8,128]{2,1,0:T(8,128)S(1)} %shard_map.97), channel_id=1, source_target_pairs={{2,0},{4,2},{6,4},{8,6},{10,8},{12,10},{14,12},{3,1},{5,3},{7,5},{... | collective-permute-start | bytes 147464 | tf_op jit(solution)/shard_map/ppermute | solution.py:26
  50.9 15.5 %copy-start = (f32[24,8,128]{2,1,0:T(8,128)S(1)}, f32[24,8,128]{2,1,0:T(8,128)}, u32[]{:S(2)}) copy-start(f32[24,8,128]{2,1,0:T(8,128)} %sol.1) | copy-start | bytes 294916

commit v2 on v1

--- a/solution.py
+++ b/solution.py
@@ -63,17 +63,22 @@
 def face_kernel(*refs):
     given, y_face, x_face, held, sems = refs[:6], refs[6], refs[7], refs[8:14], refs[14]
     n = given[0].shape[0]
-    copies = [pltpu.make_async_copy(src, dst, sems.at[a]) for a, (src, dst) in enumerate(zip(given, held))]
-    for copy in copies:
-        copy.start()
-    for copy in copies:
-        copy.wait()
+    size = n // PARTS
+    copies = []
+    for part in range(PARTS):
+        levels = pl.ds(part * size, size)
+        for a, (src, dst) in enumerate(zip(given, held)):
+            copies.append(pltpu.make_async_copy(src.at[levels], dst.at[levels], sems.at[6 * part + a]))
+            copies[-1].start()
     dirn, resid, cond_x, cond_y, cond_z, helmholtz = held
     row, col = iota(0), iota(1)
     face = 127 - 127 * lax.axis_index("gy")
     y_tiles = [jnp.zeros((8, 128), jnp.float32) for t in range(y_face.shape[0])]
     x_tiles = [jnp.zeros((8, 128), jnp.float32) for t in range(x_face.shape[0])]
     for k in range(n):
+        if k % size == 0:
+            for copy in copies[6 * (k // size):6 * (k // size) + 6]:
+                copy.wait()
         diag = partial_diagonal(k, 0.0, cond_x, cond_y, cond_z, helmholtz)
         for v, value in enumerate((dirn[k], cond_y[k], diag, cond_z[k], resid[k], cond_x[k])):
             at = k % 16 * 8 + v
@@ -326,16 +331,16 @@
     back[pl.ds(1, n, stride=BACK), :] = jnp.where(lanes <= LEFT, x2, jnp.where(in_flux, shift_to(flux, FLUX), tail))
 
 
-def scalar_kernel(tops, got, spread):
+def scalar_kernel(low, tops, got, spread):
     n = got.shape[0] // BACK
     amount = jnp.sum(got[pl.ds(0, n, stride=BACK), :], axis=0, keepdims=True)
-    for t in range(0, spread.shape[0], 3):
-        spread[t] = amount
-        spread[t + 1] = tops[0:1, :]
-        spread[t + 2] = tops[1:2, :]
-
-
-def column_kernel(low, got, resid, cond_x, cond_y, own_parts, ext_parts, far_parts, image_in, lows,
+    for t in range(spread.shape[0]):
+        spread[t, 0:1, :] = amount
+        spread[t, 1:3, :] = tops[0:2, :]
+        spread[t, 3:4, :] = amount
+
+
+def column_kernel(got, resid, cond_x, cond_y, own_parts, ext_parts, far_parts, image_in, lows,
                   precond, image_p, image_d, tops):
     core = lax.axis_index("gy")
     n = resid.shape[0]
@@ -371,24 +376,18 @@
 
 
 def update_kernel(scalars, low, cond_x, sol, resid, dirn, precond, image_p, image_d,
-                  sol_to, res_to, dir_to, sol_out, res_out, dir_out, sems):
+                  sol_out, res_out, dir_out):
     row = iota(0)
-    mates = scalars.shape[0] // 3
-    amount = scalars[0]
-    for t in range(1, mates):
-        amount = amount + scalars[3 * t]
+    amount = jnp.sum(scalars[:, 0, :], axis=0, keepdims=True)
     per_row = lax.axis_size("gy")
     mate = lax.axis_index("gx") * per_row + lax.axis_index("gy") + per_row
-    mate = jnp.minimum(mate, mates - 1)
-    x, x2 = (jnp.broadcast_to(scalars[3 * mate + v], (8, 128)) for v in (1, 2))
+    mate = jnp.minimum(mate, scalars.shape[0] - 1)
+    x, x2 = (jnp.broadcast_to(scalars[mate, v:v + 1, :], (8, 128)) for v in (1, 2))
     r_p, p_nd, p_np, d_ad, r_d = (jnp.broadcast_to(amount[:, v:v + 1], (8, 128)) for v in range(SUMS, SUMS + 5))
     p_ad = r_d - p_nd
     conj = -p_ad / d_ad
     step = (r_p + conj * r_d) / (r_p - p_np + conj * p_ad)
-    n = sol.shape[0]
-    size = n // PARTS
-    copies = []
-    for k in range(n):
+    for k in range(sol.shape[0]):
         out = precond[k] + conj * dirn[k]
         dir_out[k] = out
         sol_out[k] = sol[k] + step * out
@@ -396,21 +395,13 @@
         p_up = b_up + x * f_up + x2 * l_up
         above = jnp.where(row == 7, cond_x[k] * (p_up + conj * d_up), 0.0)
         res_out[k] = resid[k] - step * (image_p[k] + conj * image_d[k] - above)
-        if (k + 1) % size == 0:
-            part = k // size
-            levels = pl.ds(part * size, size)
-            for a, (src, dst) in enumerate(((sol_out, sol_to), (res_out, res_to), (dir_out, dir_to))):
-                copies.append(pltpu.make_async_copy(src.at[levels], dst.at[levels], sems.at[3 * part + a]))
-                copies[-1].start()
-    for copy in copies:
-        copy.wait()
-
-
-def call(kernel, outs, *args, scratch=(), first=0, out_spec=VMEM):
+
+
+def call(kernel, outs, *args, scratch=(), first=0):
     many = isinstance(outs, tuple)
     return pl.pallas_call(
         kernel, out_shape=outs, in_specs=[ANY] * first + [VMEM] * (len(args) - first),
-        out_specs=(out_spec,) * len(outs) if many else out_spec, scratch_shapes=scratch,
+        out_specs=(VMEM,) * len(outs) if many else VMEM, scratch_shapes=scratch,
         compiler_params=pltpu.CompilerParams(vmem_limit_bytes=8 << 20))(*args)
 
 
@@ -425,7 +416,7 @@
 
     y_face, x_face, *given = call(
         face_kernel, (shape(-(-nz // 16), nx, ny), shape(nz * 5 // 8, nx, ny)) + (field,) * 6, *given,
-        scratch=(pltpu.SemaphoreType.DMA((6,)),), first=6)
+        scratch=(pltpu.SemaphoreType.DMA((6 * PARTS,)),), first=6)
     direction_in, residual_in, cond_x, cond_y, cond_z, helmholtz = given
     up = shifted(x_face, "gx", 1)
     y_got = lax.ppermute(y_face, "gy", [(0, 1), (1, 0)])
@@ -441,13 +432,12 @@
     low = shifted(low, "gx", -1)
     got = lax.all_to_all(back.reshape(gz, BACK, ny), "gz", 0, 0, tiled=True).reshape(gz * BACK, ny)
     precond, image_p, image_d, tops = call(
-        column_kernel, (field, field, field, shape(8, ny)), low, got, residual_in, cond_x, cond_y,
-        own_parts, ext_parts, far_parts, image, lows, first=1)
-    sums = call(scalar_kernel, shape(mates * 3, 1, ny), tops, got)
+        column_kernel, (field, field, field, shape(8, ny)), got, residual_in, cond_x, cond_y,
+        own_parts, ext_parts, far_parts, image, lows)
+    sums = call(scalar_kernel, shape(mates, 4, ny), low, tops, got, first=1)
     sums = lax.all_to_all(sums, ("gx", "gy"), 0, 0, tiled=True)
     return call(update_kernel, (field, field, field), sums, low, cond_x, solution_in, residual_in, direction_in,
-                precond, image_p, image_d, out_spec=ANY,
-                scratch=(pltpu.VMEM((nz, nx, ny), jnp.float32),) * 3 + (pltpu.SemaphoreType.DMA((3 * PARTS,)),))
+                precond, image_p, image_d)
 
 
 def solution(mesh):

time: 67.7 us -> 67.4 us (level)
    all_to_all x1, waiting for transfers between devices: 3.6 us -> 7.43 us  [body(): lax.all_to_all(back.reshape(gz, BACK, ny), 'gz', 0, 0, tiled=True)]
    ppermute x2, waiting for transfers between devices: 3.83 us -> 0.01 us  [shifted(): lax.ppermute(value, axis, [(i, i + by) for i in range(count) if 0 <= i +...]
  transfers between devices with their start and end apart: 5 -> 5, of which waited for: 3 -> 2; matrix products, arithmetic and copies ran while one was open for 0% -> 0% of each run, Pallas kernels for 0% -> 0%
where the time goes in v2:
time: 67.4 us; the launch traced here: 67 us
  blocking collectives  36.1 us (54%)
  starting transfers between devices  17.1 us (25%)
  waiting for transfers between devices  8.23 us (12%)
  Pallas kernels  4.83 us (7%)
  between operations  0.74 us (1%)
    all_to_all x1, blocking collectives, body(): rows = lax.all_to_all(spread.reshape(gz, ROWS, ny), 'gz', 0, 0, tiled=True)  20.8 us
    all_to_all x1, blocking collectives, body(): sums = lax.all_to_all(sums, ('gx', 'gy'), 0, 0, tiled=True)  15.3 us
    all_to_all x1, waiting for transfers between devices, body(): lax.all_to_all(back.reshape(gz, BACK, ny), 'gz', 0, 0, tiled=True)  7.43 us
    ppermute x2, starting transfers between devices, shifted(): lax.ppermute(value, axis, [(i, i + by) for i in range(count) if 0 <= i +...  5.33 us
    pallas_call x7, Pallas kernels, call(): pl.pallas_call(kernel, out_shape=outs, in_specs=[ANY] * first + [VMEM] *...  4.83 us
    all_to_all x1, starting transfers between devices, body(): lax.all_to_all(back.reshape(gz, BACK, ny), 'gz', 0, 0, tiled=True)  4.43 us
    ppermute x1, starting transfers between devices, body(): lax.ppermute(y_face, ('gx', 'gy'), [(2 * i + c, 2 * i + 3 - c) for i in r...  4.04 us
    ppermute x1, starting transfers between devices, body(): y_got = lax.ppermute(y_face, 'gy', [(0, 1), (1, 0)])  3.29 us
  transfers between devices with their start and end apart: 5, of which 2 were waited for; matrix products, arithmetic and copies ran while one was open for 0% of the time, Pallas kernels for 0%

profile of v2, /device:TPU:1, one launch (start us, length us, event | category | flops | bytes accessed | tf_op | source)
XLA Modules:
  0.0 67.0 jit_solution(7918617485395258894)
XLA Ops:
  0.6 1.5 %shard_map.94 = (f32[2,8,128]{2,1,0:T(8,128)S(1)}, f32[15,8,128]{2,1,0:T(8,128)S(1)}, f32[24,8,128]{2,1,0:T(8,128)S(1)}, f32[24,8,128]{2,1,0:T(8,128)S(1)}, f32[...) custom-call(f32[24,8,128]{2,1,0:T(8,128)} %refs_0_.1, ...), custom_call_target="tpu_custom_call" | custom-call | tf_op jit(solution)/shard_map/pallas_call | solution.py:402
  2.2 4.0 %collective-permute-start.2 = (f32[15,8,128]{2,1,0:T(8,128)S(1)}, f32[15,8,128]{2,1,0:T(8,128)S(1)}, u32[]{:S(2)}, u32[]{:S(2)}) collective-permute-start(f32[15,8,128]{2,1,0:T(8,128)S(1)} %get-tuple-element.28), channel_id=1, source_target_pairs={{0,2},{2,4},{4,6},{6,8},{8,10},{10,12},{12,14},{1,3},{3,5},{5,7},{... | collective-permute-start | bytes 184328 | tf_op jit(solution)/shard_map/ppermute | solution.py:26
  6.2 4.0 %collective-permute-start.1 = (f32[2,8,128]{2,1,0:T(8,128)S(1)}, f32[2,8,128]{2,1,0:T(8,128)S(1)}, u32[]{:S(2)}, u32[]{:S(2)}) collective-permute-start(f32[2,8,128]{2,1,0:T(8,128)S(1)} %get-tuple-element.27), channel_id=1, source_target_pairs={{0,3},{1,2},{2,5},{3,4},{4,7},{5,6},{6,9},{7,8},{8,11},{9,10},{10,... | collective-permute-start | bytes 24584 | tf_op jit(solution)/shard_map/ppermute | solution.py:423
  10.2 3.3 %collective-permute-start = (f32[2,8,128]{2,1,0:T(8,128)S(1)}, f32[2,8,128]{2,1,0:T(8,128)S(1)}, u32[]{:S(2)}, u32[]{:S(2)}) collective-permute-start(f32[2,8,128]{2,1,0:T(8,128)S(1)} %get-tuple-element.27), channel_id=1, source_target_pairs={{0,1},{1,0},{2,3},{3,2},{4,5},{5,4},{6,7},{7,6},{8,9},{9,8},{10,11... | collective-permute-start | bytes 24584 | tf_op jit(solution)/shard_map/ppermute | solution.py:422
  13.5 0.0 collective-permute-done.1.diagonal_got
  13.6 0.8 %collective-permute-done.y_got = f32[2,8,128]{2,1,0:T(8,128)S(1)} collective-permute-done((f32[2,8,128]{2,1,0:T(8,128)S(1)}, f32[2,8,128]{2,1,0:T(8,128)S(1)}, u32[]{:S(2)}, u32[]{:S(2)}) %collective-permute-start) | collective-permute-done | bytes 8224 | tf_op jit(solution)/shard_map/ppermute | solution.py:422
  14.4 0.0 collective-permute-done.2.up
  14.4 1.0 %shard_map.95 = (f32[256,128]{1,0:T(8,128)S(1)}, f32[3,24,8,128]{3,2,1,0:T(8,128)S(1)}, f32[3,24,8,128]{3,2,1,0:T(8,128)S(1)}, f32[3,24,8,128]{3,2,1,0:T(8,128)S...) custom-call(f32[24,8,128]{2,1,0:T(8,128)S(1)} %get-tuple-element.21.dirn, ...), custom_call_target="tpu_custom_call" | custom-call | tf_op jit(solution)/shard_map/pallas_call | solution.py:402
  15.4 20.8 %all_to_all.15 = f32[32,8,128]{2,1,0:T(8,128)S(1)} all-to-all(f32[32,8,128]{2,1,0:T(8,128)S(1)} %bitcast.7), channel_id=1, replica_groups=mesh['gz'=32,'gx'=8,'gy'=2] {'gz'}, dimensions={0} | all-to-all | bytes 262144 | tf_op jit(solution)/shard_map/all_to_all | solution.py:428
  36.2 1.2 %shard_map.96.back = f32[64,128]{1,0:T(8,128)} custom-call(f32[256,128]{1,0:T(8,128)S(1)} %bitcast.4), custom_call_target="tpu_custom_call" | custom-call | tf_op jit(solution)/shard_map/pallas_call | solution.py:402
  37.4 4.4 %all-to-all-start.1 = ((f32[32,2,128]{2,1,0:T(2,128)}), f32[32,2,128]{2,1,0:T(2,128)S(1)}, u32[]{:S(2)}, u32[]{:S(2)}) async-start(f32[32,2,128]{2,1,0:T(2,128)} %bitcast.2), calls=%async_computation.1 | async-start | bytes 65536 | tf_op jit(solution)/shard_map/all_to_all | solution.py:433
  41.9 1.3 %collective-permute-start.3 = (f32[12,8,128]{2,1,0:T(8,128)S(1)}, f32[12,8,128]{2,1,0:T(8,128)S(1)}, u32[]{:S(2)}, u32[]{:S(2)}) collective-permute-start(f32[12,8,128]{2,1,0:T(8,128)S(1)} %shard_map.97), channel_id=1, source_target_pairs={{2,0},{4,2},{6,4},{8,6},{10,8},{12,10},{14,12},{3,1},{5,3},{7,5},{... | collective-permute-start | bytes 147464 | tf_op jit(solution)/shard_map/ppermute | solution.py:26
  43.2 7.4 %all-to-all-done.1 = f32[32,2,128]{2,1,0:T(2,128)S(1)} async-done(((f32[32,2,128]{2,1,0:T(2,128)}), f32[32,2,128]{2,1,0:T(2,128)S(1)}, u32[]{:S(2)}, u32[]{:S(2)}) %all-to-all-start.1) | async-done | bytes 32800 | tf_op jit(solution)/shard_map/all_to_all | solution.py:433
  50.6 0.2 shard_map.98
  50.8 0.0 copy-start
  50.8 0.0 collective-permute-done.3.low
  50.8 15.3 %all_to_all.16.scalars = f32[16,4,128]{2,1,0:T(4,128)S(1)} all-to-all(f32[16,4,128]{2,1,0:T(4,128)S(1)} %shard_map.99), channel_id=1, replica_groups=mesh['gz'=32,'gx'=8,'gy'=2] {'gx','gy'}, dimensions={0} | all-to-all | bytes 65536 | tf_op jit(solution)/shard_map/all_to_all | solution.py:438
  66.2 0.0 copy-done
  66.2 0.8 %shard_map.100 = (f32[24,8,128]{2,1,0:T(8,128)}, f32[24,8,128]{2,1,0:T(8,128)}, f32[24,8,128]{2,1,0:T(8,128)}) custom-call(f32[16,4,128]{2,1,0:T(4,128)S(1)} %all_to_all.16.scalars, f32[12,8,128]{2,1,0:T(8,128)S(1)} %collective-permute-done.3.low, f32[24,8,128]{2,1,0:T(8,128)S(1)} %get-tuple-element.23.cond_x, f32[24,8,128]{2,1,0:T(8,128)S(1)} %copy-done, ...), custom_call_target="tpu_custom_call" | custom-call | tf_op jit(solution)/shard_map/pallas_call | solution.py:402
  (2 shorter events, 0.1 us)
Async XLA Ops:
  2.2 12.2 %collective-permute-start.2 = (f32[15,8,128]{2,1,0:T(8,128)S(1)}, f32[15,8,128]{2,1,0:T(8,128)S(1)}, u32[]{:S(2)}, u32[]{:S(2)}) collective-permute-start(f32[15,8,128]{2,1,0:T(8,128)S(1)} %get-tuple-element.28), channel_id=1, source_target_pairs={{0,2},{2,4},{4,6},{6,8},{8,10},{10,12},{12,14},{1,3},{3,5},{5,7},{... | collective-permute-start | bytes 184328 | tf_op jit(solution)/shard_map/ppermute | solution.py:26
  6.2 7.4 %collective-permute-start.1 = (f32[2,8,128]{2,1,0:T(8,128)S(1)}, f32[2,8,128]{2,1,0:T(8,128)S(1)}, u32[]{:S(2)}, u32[]{:S(2)}) collective-permute-start(f32[2,8,128]{2,1,0:T(8,128)S(1)} %get-tuple-element.27), channel_id=1, source_target_pairs={{0,3},{1,2},{2,5},{3,4},{4,7},{5,6},{6,9},{7,8},{8,11},{9,10},{10,... | collective-permute-start | bytes 24584 | tf_op jit(solution)/shard_map/ppermute | solution.py:423
  10.2 4.1 %collective-permute-start = (f32[2,8,128]{2,1,0:T(8,128)S(1)}, f32[2,8,128]{2,1,0:T(8,128)S(1)}, u32[]{:S(2)}, u32[]{:S(2)}) collective-permute-start(f32[2,8,128]{2,1,0:T(8,128)S(1)} %get-tuple-element.27), channel_id=1, source_target_pairs={{0,1},{1,0},{2,3},{3,2},{4,5},{5,4},{6,7},{7,6},{8,9},{9,8},{10,11... | collective-permute-start | bytes 24584 | tf_op jit(solution)/shard_map/ppermute | solution.py:422
  37.4 13.2 %all-to-all-start.1 = ((f32[32,2,128]{2,1,0:T(2,128)}), f32[32,2,128]{2,1,0:T(2,128)S(1)}, u32[]{:S(2)}, u32[]{:S(2)}) async-start(f32[32,2,128]{2,1,0:T(2,128)} %bitcast.2), calls=%async_computation.1 | async-start | bytes 65536 | tf_op jit(solution)/shard_map/all_to_all | solution.py:433
  41.9 8.9 %collective-permute-start.3 = (f32[12,8,128]{2,1,0:T(8,128)S(1)}, f32[12,8,128]{2,1,0:T(8,128)S(1)}, u32[]{:S(2)}, u32[]{:S(2)}) collective-permute-start(f32[12,8,128]{2,1,0:T(8,128)S(1)} %shard_map.97), channel_id=1, source_target_pairs={{2,0},{4,2},{6,4},{8,6},{10,8},{12,10},{14,12},{3,1},{5,3},{7,5},{... | collective-permute-start | bytes 147464 | tf_op jit(solution)/shard_map/ppermute | solution.py:26
  50.8 15.4 %copy-start = (f32[24,8,128]{2,1,0:T(8,128)S(1)}, f32[24,8,128]{2,1,0:T(8,128)}, u32[]{:S(2)}) copy-start(f32[24,8,128]{2,1,0:T(8,128)} %sol.1) | copy-start | bytes 294916

commit v3 on v2

--- a/solution.py
+++ b/solution.py
@@ -5,7 +5,7 @@
 from jax.experimental.pallas import tpu as pltpu
 from jax.sharding import PartitionSpec as P
 
-PARTS = 3
+PARTS = 2
 QUARTERS = 4
 WIDTH = 128 // QUARTERS
 ROWS = 8
@@ -331,7 +331,7 @@
     back[pl.ds(1, n, stride=BACK), :] = jnp.where(lanes <= LEFT, x2, jnp.where(in_flux, shift_to(flux, FLUX), tail))
 
 
-def scalar_kernel(low, tops, got, spread):
+def scalar_kernel(tops, got, spread):
     n = got.shape[0] // BACK
     amount = jnp.sum(got[pl.ds(0, n, stride=BACK), :], axis=0, keepdims=True)
     for t in range(spread.shape[0]):
@@ -340,7 +340,7 @@
         spread[t, 3:4, :] = amount
 
 
-def column_kernel(got, resid, cond_x, cond_y, own_parts, ext_parts, far_parts, image_in, lows,
+def column_kernel(low, got, resid, cond_x, cond_y, own_parts, ext_parts, far_parts, image_in, lows,
                   precond, image_p, image_d, tops):
     core = lax.axis_index("gy")
     n = resid.shape[0]
@@ -432,9 +432,9 @@
     low = shifted(low, "gx", -1)
     got = lax.all_to_all(back.reshape(gz, BACK, ny), "gz", 0, 0, tiled=True).reshape(gz * BACK, ny)
     precond, image_p, image_d, tops = call(
-        column_kernel, (field, field, field, shape(8, ny)), got, residual_in, cond_x, cond_y,
-        own_parts, ext_parts, far_parts, image, lows)
-    sums = call(scalar_kernel, shape(mates, 4, ny), low, tops, got, first=1)
+        column_kernel, (field, field, field, shape(8, ny)), low, got, residual_in, cond_x, cond_y,
+        own_parts, ext_parts, far_parts, image, lows, first=1)
+    sums = call(scalar_kernel, shape(mates, 4, ny), tops, got)
     sums = lax.all_to_all(sums, ("gx", "gy"), 0, 0, tiled=True)
     return call(update_kernel, (field, field, field), sums, low, cond_x, solution_in, residual_in, direction_in,
                 precond, image_p, image_d)

time: 67.4 us -> 67.3 us (level)
    all_to_all x1, waiting for transfers between devices: 7.43 us -> 3.6 us  [body(): lax.all_to_all(back.reshape(gz, BACK, ny), 'gz', 0, 0, tiled=True)]
    ppermute x2, waiting for transfers between devices: 0.01 us -> 3.83 us  [shifted(): lax.ppermute(value, axis, [(i, i + by) for i in range(count) if 0 <= i +...]
  transfers between devices with their start and end apart: 5 -> 5, of which waited for: 2 -> 3; matrix products, arithmetic and copies ran while one was open for 0% -> 0% of each run, Pallas kernels for 0% -> 0%
where the time goes in v3:
time: 67.3 us; the launch traced here: 66.9 us
  blocking collectives  36.1 us (54%)
  starting transfers between devices  17.1 us (25%)
  waiting for transfers between devices  8.23 us (12%)
  Pallas kernels  4.72 us (7%)
  between operations  0.73 us (1%)
    all_to_all x1, blocking collectives, body(): rows = lax.all_to_all(spread.reshape(gz, ROWS, ny), 'gz', 0, 0, tiled=True)  20.8 us
    all_to_all x1, blocking collectives, body(): sums = lax.all_to_all(sums, ('gx', 'gy'), 0, 0, tiled=True)  15.3 us
    ppermute x2, starting transfers between devices, shifted(): lax.ppermute(value, axis, [(i, i + by) for i in range(count) if 0 <= i +...  5.33 us
    pallas_call x7, Pallas kernels, call(): pl.pallas_call(kernel, out_shape=outs, in_specs=[ANY] * first + [VMEM] *...  4.72 us
    all_to_all x1, starting transfers between devices, body(): lax.all_to_all(back.reshape(gz, BACK, ny), 'gz', 0, 0, tiled=True)  4.43 us
    ppermute x1, starting transfers between devices, body(): lax.ppermute(y_face, ('gx', 'gy'), [(2 * i + c, 2 * i + 3 - c) for i in r...  4.04 us
    ppermute x2, waiting for transfers between devices, shifted(): lax.ppermute(value, axis, [(i, i + by) for i in range(count) if 0 <= i +...  3.83 us
    all_to_all x1, waiting for transfers between devices, body(): lax.all_to_all(back.reshape(gz, BACK, ny), 'gz', 0, 0, tiled=True)  3.6 us
  transfers between devices with their start and end apart: 5, of which 3 were waited for; matrix products, arithmetic and copies ran while one was open for 0% of the time, Pallas kernels for 0%

profile of v3, /device:TPU:1, one launch (start us, length us, event | category | flops | bytes accessed | tf_op | source)
XLA Modules:
  0.0 66.9 jit_solution(1656575762457993557)
XLA Ops:
  0.6 1.4 %shard_map.94 = (f32[2,8,128]{2,1,0:T(8,128)S(1)}, f32[15,8,128]{2,1,0:T(8,128)S(1)}, f32[24,8,128]{2,1,0:T(8,128)S(1)}, f32[24,8,128]{2,1,0:T(8,128)S(1)}, f32[...) custom-call(f32[24,8,128]{2,1,0:T(8,128)} %refs_0_.1, ...), custom_call_target="tpu_custom_call" | custom-call | tf_op jit(solution)/shard_map/pallas_call | solution.py:402
  2.0 4.0 %collective-permute-start.2 = (f32[15,8,128]{2,1,0:T(8,128)S(1)}, f32[15,8,128]{2,1,0:T(8,128)S(1)}, u32[]{:S(2)}, u32[]{:S(2)}) collective-permute-start(f32[15,8,128]{2,1,0:T(8,128)S(1)} %get-tuple-element.28), channel_id=1, source_target_pairs={{0,2},{2,4},{4,6},{6,8},{8,10},{10,12},{12,14},{1,3},{3,5},{5,7},{... | collective-permute-start | bytes 184328 | tf_op jit(solution)/shard_map/ppermute | solution.py:26
  6.1 4.0 %collective-permute-start.1 = (f32[2,8,128]{2,1,0:T(8,128)S(1)}, f32[2,8,128]{2,1,0:T(8,128)S(1)}, u32[]{:S(2)}, u32[]{:S(2)}) collective-permute-start(f32[2,8,128]{2,1,0:T(8,128)S(1)} %get-tuple-element.27), channel_id=1, source_target_pairs={{0,3},{1,2},{2,5},{3,4},{4,7},{5,6},{6,9},{7,8},{8,11},{9,10},{10,... | collective-permute-start | bytes 24584 | tf_op jit(solution)/shard_map/ppermute | solution.py:423
  10.1 3.3 %collective-permute-start = (f32[2,8,128]{2,1,0:T(8,128)S(1)}, f32[2,8,128]{2,1,0:T(8,128)S(1)}, u32[]{:S(2)}, u32[]{:S(2)}) collective-permute-start(f32[2,8,128]{2,1,0:T(8,128)S(1)} %get-tuple-element.27), channel_id=1, source_target_pairs={{0,1},{1,0},{2,3},{3,2},{4,5},{5,4},{6,7},{7,6},{8,9},{9,8},{10,11... | collective-permute-start | bytes 24584 | tf_op jit(solution)/shard_map/ppermute | solution.py:422
  13.4 0.0 collective-permute-done.1.diagonal_got
  13.5 0.8 %collective-permute-done.y_got = f32[2,8,128]{2,1,0:T(8,128)S(1)} collective-permute-done((f32[2,8,128]{2,1,0:T(8,128)S(1)}, f32[2,8,128]{2,1,0:T(8,128)S(1)}, u32[]{:S(2)}, u32[]{:S(2)}) %collective-permute-start) | collective-permute-done | bytes 8224 | tf_op jit(solution)/shard_map/ppermute | solution.py:422
  14.2 0.0 collective-permute-done.2.up
  14.3 1.0 %shard_map.95 = (f32[256,128]{1,0:T(8,128)S(1)}, f32[3,24,8,128]{3,2,1,0:T(8,128)S(1)}, f32[3,24,8,128]{3,2,1,0:T(8,128)S(1)}, f32[3,24,8,128]{3,2,1,0:T(8,128)S...) custom-call(f32[24,8,128]{2,1,0:T(8,128)S(1)} %get-tuple-element.21.dirn, ...), custom_call_target="tpu_custom_call" | custom-call | tf_op jit(solution)/shard_map/pallas_call | solution.py:402
  15.3 20.8 %all_to_all.15 = f32[32,8,128]{2,1,0:T(8,128)S(1)} all-to-all(f32[32,8,128]{2,1,0:T(8,128)S(1)} %bitcast.7), channel_id=1, replica_groups=mesh['gz'=32,'gx'=8,'gy'=2] {'gz'}, dimensions={0} | all-to-all | bytes 262144 | tf_op jit(solution)/shard_map/all_to_all | solution.py:428
  36.1 1.2 %shard_map.96.back = f32[64,128]{1,0:T(8,128)} custom-call(f32[256,128]{1,0:T(8,128)S(1)} %bitcast.4), custom_call_target="tpu_custom_call" | custom-call | tf_op jit(solution)/shard_map/pallas_call | solution.py:402
  37.3 4.4 %all-to-all-start.1 = ((f32[32,2,128]{2,1,0:T(2,128)}), f32[32,2,128]{2,1,0:T(2,128)S(1)}, u32[]{:S(2)}, u32[]{:S(2)}) async-start(f32[32,2,128]{2,1,0:T(2,128)} %bitcast.2), calls=%async_computation.1 | async-start | bytes 65536 | tf_op jit(solution)/shard_map/all_to_all | solution.py:433
  41.8 1.3 %collective-permute-start.3 = (f32[12,8,128]{2,1,0:T(8,128)S(1)}, f32[12,8,128]{2,1,0:T(8,128)S(1)}, u32[]{:S(2)}, u32[]{:S(2)}) collective-permute-start(f32[12,8,128]{2,1,0:T(8,128)S(1)} %shard_map.97), channel_id=1, source_target_pairs={{2,0},{4,2},{6,4},{8,6},{10,8},{12,10},{14,12},{3,1},{5,3},{7,5},{... | collective-permute-start | bytes 147464 | tf_op jit(solution)/shard_map/ppermute | solution.py:26
  43.1 3.8 %collective-permute-done.3.low = f32[12,8,128]{2,1,0:T(8,128)S(1)} collective-permute-done((f32[12,8,128]{2,1,0:T(8,128)S(1)}, f32[12,8,128]{2,1,0:T(8,128)S(1)}, u32[]{:S(2)}, u32[]{:S(2)}) %collective-permute-start.3) | collective-permute-done | bytes 49184 | tf_op jit(solution)/shard_map/ppermute | solution.py:26
  46.9 3.6 %all-to-all-done.1 = f32[32,2,128]{2,1,0:T(2,128)S(1)} async-done(((f32[32,2,128]{2,1,0:T(2,128)}), f32[32,2,128]{2,1,0:T(2,128)S(1)}, u32[]{:S(2)}, u32[]{:S(2)}) %all-to-all-start.1) | async-done | bytes 32800 | tf_op jit(solution)/shard_map/all_to_all | solution.py:433
  50.5 0.2 shard_map.98
  50.7 0.0 copy-start
  50.7 15.3 %all_to_all.16.scalars = f32[16,4,128]{2,1,0:T(4,128)S(1)} all-to-all(f32[16,4,128]{2,1,0:T(4,128)S(1)} %shard_map.99), channel_id=1, replica_groups=mesh['gz'=32,'gx'=8,'gy'=2] {'gx','gy'}, dimensions={0} | all-to-all | bytes 65536 | tf_op jit(solution)/shard_map/all_to_all | solution.py:438
  66.1 0.0 copy-done
  66.1 0.8 %shard_map.100 = (f32[24,8,128]{2,1,0:T(8,128)}, f32[24,8,128]{2,1,0:T(8,128)}, f32[24,8,128]{2,1,0:T(8,128)}) custom-call(f32[16,4,128]{2,1,0:T(4,128)S(1)} %all_to_all.16.scalars, f32[12,8,128]{2,1,0:T(8,128)S(1)} %collective-permute-done.3.low, f32[24,8,128]{2,1,0:T(8,128)S(1)} %get-tuple-element.23.cond_x, f32[24,8,128]{2,1,0:T(8,128)S(1)} %copy-done, ...), custom_call_target="tpu_custom_call" | custom-call | tf_op jit(solution)/shard_map/pallas_call | solution.py:402
  (2 shorter events, 0.1 us)
Async XLA Ops:
  2.0 12.2 %collective-permute-start.2 = (f32[15,8,128]{2,1,0:T(8,128)S(1)}, f32[15,8,128]{2,1,0:T(8,128)S(1)}, u32[]{:S(2)}, u32[]{:S(2)}) collective-permute-start(f32[15,8,128]{2,1,0:T(8,128)S(1)} %get-tuple-element.28), channel_id=1, source_target_pairs={{0,2},{2,4},{4,6},{6,8},{8,10},{10,12},{12,14},{1,3},{3,5},{5,7},{... | collective-permute-start | bytes 184328 | tf_op jit(solution)/shard_map/ppermute | solution.py:26
  6.1 7.4 %collective-permute-start.1 = (f32[2,8,128]{2,1,0:T(8,128)S(1)}, f32[2,8,128]{2,1,0:T(8,128)S(1)}, u32[]{:S(2)}, u32[]{:S(2)}) collective-permute-start(f32[2,8,128]{2,1,0:T(8,128)S(1)} %get-tuple-element.27), channel_id=1, source_target_pairs={{0,3},{1,2},{2,5},{3,4},{4,7},{5,6},{6,9},{7,8},{8,11},{9,10},{10,... | collective-permute-start | bytes 24584 | tf_op jit(solution)/shard_map/ppermute | solution.py:423
  10.1 4.1 %collective-permute-start = (f32[2,8,128]{2,1,0:T(8,128)S(1)}, f32[2,8,128]{2,1,0:T(8,128)S(1)}, u32[]{:S(2)}, u32[]{:S(2)}) collective-permute-start(f32[2,8,128]{2,1,0:T(8,128)S(1)} %get-tuple-element.27), channel_id=1, source_target_pairs={{0,1},{1,0},{2,3},{3,2},{4,5},{5,4},{6,7},{7,6},{8,9},{9,8},{10,11... | collective-permute-start | bytes 24584 | tf_op jit(solution)/shard_map/ppermute | solution.py:422
  37.3 13.2 %all-to-all-start.1 = ((f32[32,2,128]{2,1,0:T(2,128)}), f32[32,2,128]{2,1,0:T(2,128)S(1)}, u32[]{:S(2)}, u32[]{:S(2)}) async-start(f32[32,2,128]{2,1,0:T(2,128)} %bitcast.2), calls=%async_computation.1 | async-start | bytes 65536 | tf_op jit(solution)/shard_map/all_to_all | solution.py:433
  41.8 5.1 %collective-permute-start.3 = (f32[12,8,128]{2,1,0:T(8,128)S(1)}, f32[12,8,128]{2,1,0:T(8,128)S(1)}, u32[]{:S(2)}, u32[]{:S(2)}) collective-permute-start(f32[12,8,128]{2,1,0:T(8,128)S(1)} %shard_map.97), channel_id=1, source_target_pairs={{2,0},{4,2},{6,4},{8,6},{10,8},{12,10},{14,12},{3,1},{5,3},{7,5},{... | collective-permute-start | bytes 147464 | tf_op jit(solution)/shard_map/ppermute | solution.py:26
  50.7 15.4 %copy-start = (f32[24,8,128]{2,1,0:T(8,128)S(1)}, f32[24,8,128]{2,1,0:T(8,128)}, u32[]{:S(2)}) copy-start(f32[24,8,128]{2,1,0:T(8,128)} %sol.1) | copy-start | bytes 294916

commit v4 on v3

--- a/solution.py
+++ b/solution.py
@@ -63,10 +63,10 @@
 def face_kernel(*refs):
     given, y_face, x_face, held, sems = refs[:6], refs[6], refs[7], refs[8:14], refs[14]
     n = given[0].shape[0]
-    size = n // PARTS
+    size = 2 * n // 3
     copies = []
     for part in range(PARTS):
-        levels = pl.ds(part * size, size)
+        levels = pl.ds(0, size) if part == 0 else pl.ds(size, n - size)
         for a, (src, dst) in enumerate(zip(given, held)):
             copies.append(pltpu.make_async_copy(src.at[levels], dst.at[levels], sems.at[6 * part + a]))
             copies[-1].start()

time: 67.3 us -> 67.4 us (level)
  no operation moved by 1% of the time
where the time goes in v4:
time: 67.4 us; the launch traced here: 67 us
  blocking collectives  36.1 us (54%)
  starting transfers between devices  17.1 us (25%)
  waiting for transfers between devices  8.23 us (12%)
  Pallas kernels  4.85 us (7%)
  between operations  0.73 us (1%)
    all_to_all x1, blocking collectives, body(): rows = lax.all_to_all(spread.reshape(gz, ROWS, ny), 'gz', 0, 0, tiled=True)  20.8 us
    all_to_all x1, blocking collectives, body(): sums = lax.all_to_all(sums, ('gx', 'gy'), 0, 0, tiled=True)  15.3 us
    ppermute x2, starting transfers between devices, shifted(): lax.ppermute(value, axis, [(i, i + by) for i in range(count) if 0 <= i +...  5.33 us
    pallas_call x7, Pallas kernels, call(): pl.pallas_call(kernel, out_shape=outs, in_specs=[ANY] * first + [VMEM] *...  4.85 us
    all_to_all x1, starting transfers between devices, body(): lax.all_to_all(back.reshape(gz, BACK, ny), 'gz', 0, 0, tiled=True)  4.43 us
    ppermute x1, starting transfers between devices, body(): lax.ppermute(y_face, ('gx', 'gy'), [(2 * i + c, 2 * i + 3 - c) for i in r...  4.04 us
    ppermute x2, waiting for transfers between devices, shifted(): lax.ppermute(value, axis, [(i, i + by) for i in range(count) if 0 <= i +...  3.83 us
    all_to_all x1, waiting for transfers between devices, body(): lax.all_to_all(back.reshape(gz, BACK, ny), 'gz', 0, 0, tiled=True)  3.6 us
  transfers between devices with their start and end apart: 5, of which 3 were waited for; matrix products, arithmetic and copies ran while one was open for 0% of the time, Pallas kernels for 0%

profile of v4, /device:TPU:1, one launch (start us, length us, event | category | flops | bytes accessed | tf_op | source)
XLA Modules:
  0.0 67.0 jit_solution(5633593302747324791)
XLA Ops:
  0.6 1.5 %shard_map.94 = (f32[2,8,128]{2,1,0:T(8,128)S(1)}, f32[15,8,128]{2,1,0:T(8,128)S(1)}, f32[24,8,128]{2,1,0:T(8,128)S(1)}, f32[24,8,128]{2,1,0:T(8,128)S(1)}, f32[...) custom-call(f32[24,8,128]{2,1,0:T(8,128)} %refs_0_.1, ...), custom_call_target="tpu_custom_call" | custom-call | tf_op jit(solution)/shard_map/pallas_call | solution.py:402
  2.2 4.0 %collective-permute-start.2 = (f32[15,8,128]{2,1,0:T(8,128)S(1)}, f32[15,8,128]{2,1,0:T(8,128)S(1)}, u32[]{:S(2)}, u32[]{:S(2)}) collective-permute-start(f32[15,8,128]{2,1,0:T(8,128)S(1)} %get-tuple-element.28), channel_id=1, source_target_pairs={{0,2},{2,4},{4,6},{6,8},{8,10},{10,12},{12,14},{1,3},{3,5},{5,7},{... | collective-permute-start | bytes 184328 | tf_op jit(solution)/shard_map/ppermute | solution.py:26
  6.2 4.0 %collective-permute-start.1 = (f32[2,8,128]{2,1,0:T(8,128)S(1)}, f32[2,8,128]{2,1,0:T(8,128)S(1)}, u32[]{:S(2)}, u32[]{:S(2)}) collective-permute-start(f32[2,8,128]{2,1,0:T(8,128)S(1)} %get-tuple-element.27), channel_id=1, source_target_pairs={{0,3},{1,2},{2,5},{3,4},{4,7},{5,6},{6,9},{7,8},{8,11},{9,10},{10,... | collective-permute-start | bytes 24584 | tf_op jit(solution)/shard_map/ppermute | solution.py:423
  10.3 3.3 %collective-permute-start = (f32[2,8,128]{2,1,0:T(8,128)S(1)}, f32[2,8,128]{2,1,0:T(8,128)S(1)}, u32[]{:S(2)}, u32[]{:S(2)}) collective-permute-start(f32[2,8,128]{2,1,0:T(8,128)S(1)} %get-tuple-element.27), channel_id=1, source_target_pairs={{0,1},{1,0},{2,3},{3,2},{4,5},{5,4},{6,7},{7,6},{8,9},{9,8},{10,11... | collective-permute-start | bytes 24584 | tf_op jit(solution)/shard_map/ppermute | solution.py:422
  13.6 0.0 collective-permute-done.1.diagonal_got
  13.6 0.8 %collective-permute-done.y_got = f32[2,8,128]{2,1,0:T(8,128)S(1)} collective-permute-done((f32[2,8,128]{2,1,0:T(8,128)S(1)}, f32[2,8,128]{2,1,0:T(8,128)S(1)}, u32[]{:S(2)}, u32[]{:S(2)}) %collective-permute-start) | collective-permute-done | bytes 8224 | tf_op jit(solution)/shard_map/ppermute | solution.py:422
  14.4 0.0 collective-permute-done.2.up
  14.4 1.0 %shard_map.95 = (f32[256,128]{1,0:T(8,128)S(1)}, f32[3,24,8,128]{3,2,1,0:T(8,128)S(1)}, f32[3,24,8,128]{3,2,1,0:T(8,128)S(1)}, f32[3,24,8,128]{3,2,1,0:T(8,128)S...) custom-call(f32[24,8,128]{2,1,0:T(8,128)S(1)} %get-tuple-element.21.dirn, ...), custom_call_target="tpu_custom_call" | custom-call | tf_op jit(solution)/shard_map/pallas_call | solution.py:402
  15.4 20.8 %all_to_all.15 = f32[32,8,128]{2,1,0:T(8,128)S(1)} all-to-all(f32[32,8,128]{2,1,0:T(8,128)S(1)} %bitcast.7), channel_id=1, replica_groups=mesh['gz'=32,'gx'=8,'gy'=2] {'gz'}, dimensions={0} | all-to-all | bytes 262144 | tf_op jit(solution)/shard_map/all_to_all | solution.py:428
  36.2 1.2 %shard_map.96.back = f32[64,128]{1,0:T(8,128)} custom-call(f32[256,128]{1,0:T(8,128)S(1)} %bitcast.4), custom_call_target="tpu_custom_call" | custom-call | tf_op jit(solution)/shard_map/pallas_call | solution.py:402
  37.4 4.4 %all-to-all-start.1 = ((f32[32,2,128]{2,1,0:T(2,128)}), f32[32,2,128]{2,1,0:T(2,128)S(1)}, u32[]{:S(2)}, u32[]{:S(2)}) async-start(f32[32,2,128]{2,1,0:T(2,128)} %bitcast.2), calls=%async_computation.1 | async-start | bytes 65536 | tf_op jit(solution)/shard_map/all_to_all | solution.py:433
  41.9 1.3 %collective-permute-start.3 = (f32[12,8,128]{2,1,0:T(8,128)S(1)}, f32[12,8,128]{2,1,0:T(8,128)S(1)}, u32[]{:S(2)}, u32[]{:S(2)}) collective-permute-start(f32[12,8,128]{2,1,0:T(8,128)S(1)} %shard_map.97), channel_id=1, source_target_pairs={{2,0},{4,2},{6,4},{8,6},{10,8},{12,10},{14,12},{3,1},{5,3},{7,5},{... | collective-permute-start | bytes 147464 | tf_op jit(solution)/shard_map/ppermute | solution.py:26
  43.2 3.8 %collective-permute-done.3.low = f32[12,8,128]{2,1,0:T(8,128)S(1)} collective-permute-done((f32[12,8,128]{2,1,0:T(8,128)S(1)}, f32[12,8,128]{2,1,0:T(8,128)S(1)}, u32[]{:S(2)}, u32[]{:S(2)}) %collective-permute-start.3) | collective-permute-done | bytes 49184 | tf_op jit(solution)/shard_map/ppermute | solution.py:26
  47.0 3.6 %all-to-all-done.1 = f32[32,2,128]{2,1,0:T(2,128)S(1)} async-done(((f32[32,2,128]{2,1,0:T(2,128)}), f32[32,2,128]{2,1,0:T(2,128)S(1)}, u32[]{:S(2)}, u32[]{:S(2)}) %all-to-all-start.1) | async-done | bytes 32800 | tf_op jit(solution)/shard_map/all_to_all | solution.py:433
  50.6 0.2 shard_map.98
  50.8 0.0 copy-start
  50.9 15.3 %all_to_all.16.scalars = f32[16,4,128]{2,1,0:T(4,128)S(1)} all-to-all(f32[16,4,128]{2,1,0:T(4,128)S(1)} %shard_map.99), channel_id=1, replica_groups=mesh['gz'=32,'gx'=8,'gy'=2] {'gx','gy'}, dimensions={0} | all-to-all | bytes 65536 | tf_op jit(solution)/shard_map/all_to_all | solution.py:438
  66.2 0.0 copy-done
  66.2 0.8 %shard_map.100 = (f32[24,8,128]{2,1,0:T(8,128)}, f32[24,8,128]{2,1,0:T(8,128)}, f32[24,8,128]{2,1,0:T(8,128)}) custom-call(f32[16,4,128]{2,1,0:T(4,128)S(1)} %all_to_all.16.scalars, f32[12,8,128]{2,1,0:T(8,128)S(1)} %collective-permute-done.3.low, f32[24,8,128]{2,1,0:T(8,128)S(1)} %get-tuple-element.23.cond_x, f32[24,8,128]{2,1,0:T(8,128)S(1)} %copy-done, ...), custom_call_target="tpu_custom_call" | custom-call | tf_op jit(solution)/shard_map/pallas_call | solution.py:402
  (2 shorter events, 0.1 us)
Async XLA Ops:
  2.2 12.2 %collective-permute-start.2 = (f32[15,8,128]{2,1,0:T(8,128)S(1)}, f32[15,8,128]{2,1,0:T(8,128)S(1)}, u32[]{:S(2)}, u32[]{:S(2)}) collective-permute-start(f32[15,8,128]{2,1,0:T(8,128)S(1)} %get-tuple-element.28), channel_id=1, source_target_pairs={{0,2},{2,4},{4,6},{6,8},{8,10},{10,12},{12,14},{1,3},{3,5},{5,7},{... | collective-permute-start | bytes 184328 | tf_op jit(solution)/shard_map/ppermute | solution.py:26
  6.2 7.4 %collective-permute-start.1 = (f32[2,8,128]{2,1,0:T(8,128)S(1)}, f32[2,8,128]{2,1,0:T(8,128)S(1)}, u32[]{:S(2)}, u32[]{:S(2)}) collective-permute-start(f32[2,8,128]{2,1,0:T(8,128)S(1)} %get-tuple-element.27), channel_id=1, source_target_pairs={{0,3},{1,2},{2,5},{3,4},{4,7},{5,6},{6,9},{7,8},{8,11},{9,10},{10,... | collective-permute-start | bytes 24584 | tf_op jit(solution)/shard_map/ppermute | solution.py:423
  10.3 4.1 %collective-permute-start = (f32[2,8,128]{2,1,0:T(8,128)S(1)}, f32[2,8,128]{2,1,0:T(8,128)S(1)}, u32[]{:S(2)}, u32[]{:S(2)}) collective-permute-start(f32[2,8,128]{2,1,0:T(8,128)S(1)} %get-tuple-element.27), channel_id=1, source_target_pairs={{0,1},{1,0},{2,3},{3,2},{4,5},{5,4},{6,7},{7,6},{8,9},{9,8},{10,11... | collective-permute-start | bytes 24584 | tf_op jit(solution)/shard_map/ppermute | solution.py:422
  37.4 13.2 %all-to-all-start.1 = ((f32[32,2,128]{2,1,0:T(2,128)}), f32[32,2,128]{2,1,0:T(2,128)S(1)}, u32[]{:S(2)}, u32[]{:S(2)}) async-start(f32[32,2,128]{2,1,0:T(2,128)} %bitcast.2), calls=%async_computation.1 | async-start | bytes 65536 | tf_op jit(solution)/shard_map/all_to_all | solution.py:433
  41.9 5.1 %collective-permute-start.3 = (f32[12,8,128]{2,1,0:T(8,128)S(1)}, f32[12,8,128]{2,1,0:T(8,128)S(1)}, u32[]{:S(2)}, u32[]{:S(2)}) collective-permute-start(f32[12,8,128]{2,1,0:T(8,128)S(1)} %shard_map.97), channel_id=1, source_target_pairs={{2,0},{4,2},{6,4},{8,6},{10,8},{12,10},{14,12},{3,1},{5,3},{7,5},{... | collective-permute-start | bytes 147464 | tf_op jit(solution)/shard_map/ppermute | solution.py:26
  50.8 15.4 %copy-start = (f32[24,8,128]{2,1,0:T(8,128)S(1)}, f32[24,8,128]{2,1,0:T(8,128)}, u32[]{:S(2)}) copy-start(f32[24,8,128]{2,1,0:T(8,128)} %sol.1) | copy-start | bytes 294916
